TPU v7x, 256 devices: a whole 4x4x8 slice. The times are simulated.
256 devices in a mesh: subset: 16 (over x, z_lo, core), slab: 16 (over y, z_hi).
Axes of the slice: x: 4, y: 4, z: 8 (z_hi: 4, z_lo: 2; z = z_hi * 2 + z_lo), core: 2. Of those that a mesh axis runs over, the one named last changes fastest.
Arguments:
- sinogram: bfloat16 [512, 128, 2048], P(('subset', 'slab')), may hold values from -12 to 12
- angles: float32 [512], P(('subset', 'slab')), may hold values from -3.140625 to 3.140625
- w_first: float32 [32, 27], replicated, may hold values from -1.25 to 1.25
- b_first: float32 [32], replicated, may hold values from -3 to 3
- w_second: float32 [32, 27], replicated, may hold values from -0.21875 to 0.21875
- b_second: float32 [1], replicated, may hold values from -3 to 3
Outputs:
- prediction: float32 [16, 64, 8, 1024], P('subset', 'slab')
- target_slab: float32 [16, 64, 8, 1024], P('subset', 'slab')
- loss: float32 [], replicated
- grad_w_first: float32 [32, 27], replicated
- grad_b_first: float32 [32], replicated
- grad_w_second: float32 [32, 27], replicated
- grad_b_second: float32 [1], replicated
All inputs are finite; a program needn't handle non-finite values.
Results may differ from a plain program's by a relative error of at most 0.00065.
The roundings to bfloat16 on the way count: a program that leaves them out, or rounds other values in their place, can miss the bound.
Values may be sent and summed in bfloat16 or wider, within the bound.
A program may use at most 128 MiB of HBM per device.

v0:
```python
import functools
import math

import jax
import jax.numpy as jnp
from jax import lax
from jax.sharding import Mesh
from jax.sharding import PartitionSpec as P

DET = 2048
X = 1024
Y = 8
SUBSET = ("subset_0", "subset_1", "subset_2")
SLAB = ("slab_0", "slab_1")
SUBSET_SLAB = ("subset_0", "subset_1", "subset_2", "slab_0", "slab_1")


def from_partner(value, axis, apart):
    mask = 2**apart
    pairs = [(source, source ^ mask) for source in range(lax.axis_size(axis))]
    return lax.ppermute(value, axis, pairs)


def sent_to_all(value, axis):
    devices = lax.axis_size(axis)
    return lax.all_to_all(
        jnp.broadcast_to(value[None], (devices, *value.shape)), axis, 0, 0, tiled=True
    )


def taken_together(value, axis):
    return sent_to_all(value, axis).sum(axis=0)


def extended_2(value, sides, width):
    for axis, dim in sides:
        devices, length = (lax.axis_size(axis), value.shape[dim])
        up = [(i, (i + 1) % devices) for i in range(devices)]
        down = [(j, i) for i, j in up]
        last = lax.slice_in_dim(value, length - width, length, axis=dim)
        initial = lax.slice_in_dim(value, 0, width, axis=dim)
        before = lax.ppermute(last, axis, up)
        after = lax.ppermute(initial, axis, down)
        value = jnp.concatenate([before, value, after], axis=dim)
    return value


def one_axis_at_a_time(value, axes):
    return functools.reduce(lax.psum, axes, value)


def make_patches(field_pad, depth):
    rows = field_pad.shape[1]
    cols = field_pad.shape[2]
    padded = jnp.pad(field_pad, ((0, 0), (1, 1), (1, 1)))
    pieces = []
    for shift_z in range(3):
        for shift_y in range(3):
            for shift_x in range(3):
                pieces.append(
                    padded[
                        shift_z : shift_z + depth,
                        shift_y : shift_y + rows,
                        shift_x : shift_x + cols,
                    ].reshape(-1)
                )
    return jnp.stack(pieces)


def conv_second(hidden_pad, w_second, depth, rows, cols):
    channels = hidden_pad.shape[0]
    taps = jnp.dot(w_second.T, hidden_pad.reshape(channels, -1), precision=lax.Precision.HIGHEST)
    taps = taps.reshape(27, depth + 2, rows + 2, cols + 2)
    added = jnp.zeros((depth, rows, cols), jnp.float32)
    for shift_z in range(3):
        for shift_y in range(3):
            for shift_x in range(3):
                added = (
                    added
                    + taps[
                        9 * shift_z + 3 * shift_y + shift_x,
                        shift_z : shift_z + depth,
                        shift_y : shift_y + rows,
                        shift_x : shift_x + cols,
                    ]
                )
    return added


def backproject(sino, angle_vec, group):
    count_rows = sino.shape[1]
    columns = jnp.arange(X, dtype=jnp.float32) - (X - 1) / 2.0
    detector = jnp.arange(DET, dtype=jnp.float32)

    def one_group(group_index, running):
        cosines = jnp.cos(angle_vec)
        sines = jnp.sin(angle_vec)

        def one_row(row_index, inner):
            row_pos = row_index.astype(jnp.float32) - (Y - 1) / 2.0
            positions = (
                columns[None, :] * cosines[:, None] + row_pos * sines[:, None] + (DET - 1) / 2.0
            )
            weights = jnp.maximum(0.0, 1.0 - jnp.abs(positions[:, :, None] - detector)).astype(
                jnp.bfloat16
            )
            part_row = lax.dot_general(
                sino, weights, (((0, 2), (0, 2)), ((), ())), preferred_element_type=jnp.float32
            )
            start_at = (jnp.int32(0), row_index.astype(jnp.int32), jnp.int32(0))
            previous = lax.dynamic_slice(inner, start_at, (count_rows, 1, X))
            return lax.dynamic_update_slice(inner, previous + part_row[:, None, :], start_at)

        return lax.fori_loop(0, Y, one_row, running)

    empty = jnp.zeros((count_rows, Y, X), jnp.float32)
    return lax.fori_loop(0, sino.shape[0] // group, one_group, empty)


def rim_ends(extended, dim, width):
    size = extended.shape[dim]
    lower = lax.slice_in_dim(extended, 0, width, axis=dim)
    upper = lax.slice_in_dim(extended, size - width, size, axis=dim)
    return jnp.concatenate([lower, upper], axis=dim)


def join_rim(extended, received, dim, width, at_low, at_high):
    size = extended.shape[dim]
    lower = lax.slice_in_dim(extended, 0, width, axis=dim)
    middle = lax.slice_in_dim(extended, width, size - width, axis=dim)
    upper = lax.slice_in_dim(extended, size - width, size, axis=dim)
    lower = jnp.where(at_low, lax.slice_in_dim(received, 0, width, axis=dim), lower)
    upper = jnp.where(at_high, lax.slice_in_dim(received, width, 2 * width, axis=dim), upper)
    return jnp.concatenate([lower, middle, upper], axis=dim)


def body(sinogram, angles, w_first, b_first, w_second, b_second):
    n_sub = lax.axis_size(SUBSET) // 2
    n_slab = lax.axis_size(SLAB)
    local_views = sinogram.shape[0]
    depth = sinogram.shape[1] // (2 * n_slab)
    channels = w_first.shape[0]
    scale = math.pi / (local_views * n_slab * 2)
    half = lax.axis_index(SUBSET) % 2
    slab_pos = lax.axis_index(SLAB)
    z_base = (half * n_slab + slab_pos) * depth
    z_count = 2 * depth * n_slab
    at_low = (half == 1) & (slab_pos == 0)
    at_high = (half == 0) & (slab_pos == n_slab - 1)

    def inside(width):
        global_slice = z_base - width + jnp.arange(depth + 2 * width, dtype=jnp.int32)
        return ((global_slice >= 0) & (global_slice < z_count)).astype(jnp.float32)

    sino_order = (
        sinogram.reshape(local_views, 2, n_slab, depth, DET)
        .transpose(0, 2, 1, 3, 4)
        .reshape(local_views, z_count, DET)
    )
    summed = lax.psum_scatter(
        backproject(sino_order, angles, local_views), SLAB, scatter_dimension=0, tiled=True
    )
    halves = summed.reshape(2, depth, Y, X)
    mine = lax.dynamic_index_in_dim(halves, half, 0, keepdims=False)
    other = lax.dynamic_index_in_dim(halves, 1 - half, 0, keepdims=False)
    received = from_partner(other, SUBSET, 0)
    own = (mine + received) * scale
    totals = taken_together(halves, SUBSET)
    total = lax.dynamic_index_in_dim(totals, half, 0, keepdims=False) * scale
    target = (total - own) / (n_sub - 1)
    inp_ext = extended_2(own, ((SLAB, 0),), 1)
    inp_recv = from_partner(rim_ends(inp_ext, 0, 1), SUBSET, 0)
    inp_pad = join_rim(inp_ext, inp_recv, 0, 1, at_low, at_high) * inside(1)[:, None, None]
    patches = make_patches(inp_pad, depth)
    pre_act = jnp.dot(w_first, patches, precision=lax.Precision.HIGHEST) + b_first[:, None]
    hidden = jnp.maximum(pre_act, 0.0).reshape(channels, depth, Y, X)
    hidden_ext = extended_2(hidden, ((SLAB, 1),), 1)
    hidden_recv = from_partner(rim_ends(hidden_ext, 1, 1), SUBSET, 0)
    hidden_halo = (
        join_rim(hidden_ext, hidden_recv, 1, 1, at_low, at_high) * inside(1)[None, :, None, None]
    )
    hidden_pad = jnp.pad(hidden_halo, ((0, 0), (0, 0), (1, 1), (1, 1)))
    added = conv_second(hidden_pad, w_second, depth, Y, X)
    pred = own + added + b_second[0]
    cells_all = float(n_sub * z_count * Y * X)
    diff = pred - target
    loss_term = jnp.sum(diff * diff) / cells_all
    resid_grad = 2.0 * diff / cells_all
    resid_ext = extended_2(resid_grad, ((SLAB, 0),), 1)
    resid_recv = from_partner(rim_ends(resid_ext, 0, 1), SUBSET, 0)
    resid_halo = join_rim(resid_ext, resid_recv, 0, 1, at_low, at_high) * inside(1)[:, None, None]
    resid_pad = jnp.pad(resid_halo, ((0, 0), (1, 1), (1, 1)))
    resid_big = jnp.pad(resid_grad, ((2, 2), (2, 2), (2, 2)))
    near_pieces = []
    wide_pieces = []
    for shift_z in range(3):
        for shift_y in range(3):
            for shift_x in range(3):
                near_pieces.append(
                    resid_pad[
                        2 - shift_z : 2 - shift_z + depth,
                        2 - shift_y : 2 - shift_y + Y,
                        2 - shift_x : 2 - shift_x + X,
                    ].reshape(-1)
                )
                wide_pieces.append(
                    resid_big[
                        2 - shift_z : 4 - shift_z + depth,
                        2 - shift_y : 4 - shift_y + Y,
                        2 - shift_x : 4 - shift_x + X,
                    ].reshape(-1)
                )
    near_patches = jnp.stack(near_pieces)
    wide_patches = jnp.stack(wide_pieces)
    grad_hidden = jnp.dot(w_second, near_patches, precision=lax.Precision.HIGHEST)
    grad_w2 = jnp.dot(
        hidden_pad.reshape(channels, -1), wide_patches.T, precision=lax.Precision.HIGHEST
    )
    grad_pre = grad_hidden * (pre_act > 0.0).astype(jnp.float32)
    grad_w1 = jnp.dot(grad_pre, patches.T, precision=lax.Precision.HIGHEST)
    grad_b1 = jnp.sum(grad_pre, axis=1)
    grad_b2 = jnp.sum(resid_grad).reshape(1)
    loss, grad_w1, grad_b1, grad_w2, grad_b2 = (
        one_axis_at_a_time(loss_term, SUBSET_SLAB),
        one_axis_at_a_time(grad_w1, SUBSET_SLAB),
        one_axis_at_a_time(grad_b1, SUBSET_SLAB),
        one_axis_at_a_time(grad_w2, SUBSET_SLAB),
        one_axis_at_a_time(grad_b2, SUBSET_SLAB),
    )
    return (pred[None], target[None], loss, grad_w1, grad_b1, grad_w2, grad_b2)


def solution(mesh):
    finer = Mesh(
        mesh.devices.reshape(4, 2, 2, 4, 4),
        ("subset_0", "subset_1", "subset_2", "slab_0", "slab_1"),
    )
    return jax.shard_map(
        body,
        mesh=finer,
        in_specs=(P(SUBSET_SLAB, None, None), P(SUBSET_SLAB), P(), P(), P(), P()),
        out_specs=(
            P(SUBSET, SLAB, None, None),
            P(SUBSET, SLAB, None, None),
            P(),
            P(),
            P(),
            P(),
            P(),
        ),
        check_vma=False,
    )
```

profile of v0, /device:TPU:32, one launch (start us, length us, event | category | flops | bytes accessed | tf_op | source)
XLA Modules:
  0.0 644.0 jit_solution(1178662686171179533)
XLA Ops:
  12.7 140.4 %while.23 = (s32[]{:T(128)}, f32[128,8,1024]{2,1,0:T(8,128)}, f32[2]{0:T(128)S(1)}, f32[2]{0:T(128)S(1)}, bf16[2,128,2048]{2,1,0:T(8,128)(2,1)S(1)}, /*index=5*/s32[]{:T(128)}, f32[]{:T(128)}, s32[]{:T(128)}) while((s32[]{:T(128)}, f32[128,8,1024]{2,1,0:T(8,128)}, f32[2]{0:T(128)S(1)}, f32[2]{0:T(128)S(1)}, ...), condition=%wide.region_1.2_spmd.clone, body=%wide.region_0.1_spmd.clone.sunk | while | flops 1094851584 | bytes 6316189 | solution.py:114
  19.4 10.9 %dynamic_update_slice.12 = f32[128,8,1024]{2,1,0:T(8,128)} dynamic-update-slice(f32[128,8,1024]{2,1,0:T(8,128)} %get-tuple-element.402, f32[128,1,1024]{2,1,0:T(1,128)S(1)} %copy.38, s32[]{:T(128)} %constant.133.clone.1..sunk, s32[]{:T(128)S(6)} %copy.42, s32[]{:T(128)} %constant.133.clone.1..sunk) | dynamic-update-slice | bytes 1048580 | tf_op jit(solution)/shard_map/while/body/eval_jaxpr/while/body/eval_jaxpr/dynamic_update_slice | solution.py:112
  36.9 10.9 %dynamic_update_slice.12 = f32[128,8,1024]{2,1,0:T(8,128)} dynamic-update-slice(f32[128,8,1024]{2,1,0:T(8,128)} %get-tuple-element.402, f32[128,1,1024]{2,1,0:T(1,128)S(1)} %copy.38, s32[]{:T(128)} %constant.133.clone.1..sunk, s32[]{:T(128)S(6)} %copy.42, s32[]{:T(128)} %constant.133.clone.1..sunk) | dynamic-update-slice | bytes 1048580 | tf_op jit(solution)/shard_map/while/body/eval_jaxpr/while/body/eval_jaxpr/dynamic_update_slice | solution.py:112
  54.5 10.9 %dynamic_update_slice.12 = f32[128,8,1024]{2,1,0:T(8,128)} dynamic-update-slice(f32[128,8,1024]{2,1,0:T(8,128)} %get-tuple-element.402, f32[128,1,1024]{2,1,0:T(1,128)S(1)} %copy.38, s32[]{:T(128)} %constant.133.clone.1..sunk, s32[]{:T(128)S(6)} %copy.42, s32[]{:T(128)} %constant.133.clone.1..sunk) | dynamic-update-slice | bytes 1048580 | tf_op jit(solution)/shard_map/while/body/eval_jaxpr/while/body/eval_jaxpr/dynamic_update_slice | solution.py:112
  72.0 10.9 %dynamic_update_slice.12 = f32[128,8,1024]{2,1,0:T(8,128)} dynamic-update-slice(f32[128,8,1024]{2,1,0:T(8,128)} %get-tuple-element.402, f32[128,1,1024]{2,1,0:T(1,128)S(1)} %copy.38, s32[]{:T(128)} %constant.133.clone.1..sunk, s32[]{:T(128)S(6)} %copy.42, s32[]{:T(128)} %constant.133.clone.1..sunk) | dynamic-update-slice | bytes 1048580 | tf_op jit(solution)/shard_map/while/body/eval_jaxpr/while/body/eval_jaxpr/dynamic_update_slice | solution.py:112
  89.6 10.9 %dynamic_update_slice.12 = f32[128,8,1024]{2,1,0:T(8,128)} dynamic-update-slice(f32[128,8,1024]{2,1,0:T(8,128)} %get-tuple-element.402, f32[128,1,1024]{2,1,0:T(1,128)S(1)} %copy.38, s32[]{:T(128)} %constant.133.clone.1..sunk, s32[]{:T(128)S(6)} %copy.42, s32[]{:T(128)} %constant.133.clone.1..sunk) | dynamic-update-slice | bytes 1048580 | tf_op jit(solution)/shard_map/while/body/eval_jaxpr/while/body/eval_jaxpr/dynamic_update_slice | solution.py:112
  107.1 10.9 %dynamic_update_slice.12 = f32[128,8,1024]{2,1,0:T(8,128)} dynamic-update-slice(f32[128,8,1024]{2,1,0:T(8,128)} %get-tuple-element.402, f32[128,1,1024]{2,1,0:T(1,128)S(1)} %copy.38, s32[]{:T(128)} %constant.133.clone.1..sunk, s32[]{:T(128)S(6)} %copy.42, s32[]{:T(128)} %constant.133.clone.1..sunk) | dynamic-update-slice | bytes 1048580 | tf_op jit(solution)/shard_map/while/body/eval_jaxpr/while/body/eval_jaxpr/dynamic_update_slice | solution.py:112
  124.7 10.9 %dynamic_update_slice.12 = f32[128,8,1024]{2,1,0:T(8,128)} dynamic-update-slice(f32[128,8,1024]{2,1,0:T(8,128)} %get-tuple-element.402, f32[128,1,1024]{2,1,0:T(1,128)S(1)} %copy.38, s32[]{:T(128)} %constant.133.clone.1..sunk, s32[]{:T(128)S(6)} %copy.42, s32[]{:T(128)} %constant.133.clone.1..sunk) | dynamic-update-slice | bytes 1048580 | tf_op jit(solution)/shard_map/while/body/eval_jaxpr/while/body/eval_jaxpr/dynamic_update_slice | solution.py:112
  142.2 10.9 %dynamic_update_slice.12 = f32[128,8,1024]{2,1,0:T(8,128)} dynamic-update-slice(f32[128,8,1024]{2,1,0:T(8,128)} %get-tuple-element.402, f32[128,1,1024]{2,1,0:T(1,128)S(1)} %copy.38, s32[]{:T(128)} %constant.133.clone.1..sunk, s32[]{:T(128)S(6)} %copy.42, s32[]{:T(128)} %constant.133.clone.1..sunk) | dynamic-update-slice | bytes 1048580 | tf_op jit(solution)/shard_map/while/body/eval_jaxpr/while/body/eval_jaxpr/dynamic_update_slice | solution.py:112
  153.2 97.7 %reduce-scatter.2.cloned.1.call-done = f32[8,8,1024]{2,1,0:T(8,128)} async-done(((f32[128,8,1024]{2,1,0:T(8,128)}), f32[8,8,1024]{2,1,0:T(8,128)}) %reduce-scatter.2.cloned.1.call-update) | async-done | bytes 262160 | tf_op jit(solution)/shard_map/reduce_scatter | solution.py:160
  270.1 40.6 %collective-permute-done.2 = f32[1,8,1024]{2,1,0:T(8,128)S(1)} collective-permute-done((f32[1,8,1024]{2,1,0:T(8,128)S(1)}, f32[1,8,1024]{2,1,0:T(8,128)S(1)}, u32[]{:S(2)}, u32[]{:S(2)}) %collective-permute-start.2) | collective-permute-done | bytes 32800 | tf_op jit(solution)/shard_map/ppermute | solution.py:43
  322.0 10.6 %stack.9 = f32[27,32768]{1,0:T(8,128)} concatenate(f32[1,32768]{1,0:T(1,128)S(1)} %stack_reshape.243, f32[1,32768]{1,0:T(1,128)S(1)} %stack_reshape.244, f32[1,32768]{1,0:T(1,128)S(1)} %stack_reshape.245, f32[1,32768]{1,0:T(1,128)S(1)} %stack_reshape.246, f32[1,32768]{1,0:T(1,128)S(1)} %stack_reshape.247, f32[1,32768]{1,0:T(1,128)S(1)} %stack_reshape.248, ...), dimensions={0} | concatenate | bytes 7077888 | tf_op jit(solution)/shard_map/stack | solution.py:67
  349.5 37.9 %collective-permute-done.4 = f32[32,1,8,1024]{3,2,1,0:T(8,128)S(1)} collective-permute-done((f32[32,1,8,1024]{3,2,1,0:T(8,128)S(1)}, f32[32,1,8,1024]{3,2,1,0:T(8,128)S(1)}, u32[]{:S(2)}, u32[]{:S(2)}) %collective-permute-start.4) | collective-permute-done | bytes 1048608 | tf_op jit(solution)/shard_map/ppermute | solution.py:42
  400.1 9.1 %pad.16 = f32[32,6,10,1026]{3,2,1,0:T(8,128)} pad(f32[32,6,8,1024]{3,2,1,0:T(8,128)S(1)} %maximum_multiply_fusion, f32[]{:T(128)} %constant.134.clone.1), padding=0_0x0_0x1_1x1_1 | pad | bytes 14171140 | tf_op jit(solution)/shard_map/jit(_pad)/pad | solution.py:182
  409.2 10.1 %reshape.118 = f32[32,61560]{1,0:T(8,128)} reshape(f32[32,6,10,1026]{3,2,1,0:T(8,128)} %pad.16) | data formatting | bytes 15759360 | tf_op jit(solution)/shard_map/reshape | solution.py:72
  419.3 11.1 %convolution_bitcast_fusion = f32[27,61560]{1,0:T(8,128)} fusion(f32[32,61560]{1,0:T(8,128)} %reshape.118, f32[32,27]{1,0:T(8,128)S(1)} %copy-done), kind=kOutput, calls=%fused_computation.16 | convolution fusion | flops 638254080 | bytes 14531616 | tf_op jit(solution)/shard_map/dot_general | solution.py:72
  430.4 10.3 %reshape.119 = f32[27,6,10,1026]{3,2,1,0:T(8,128)} reshape(f32[27,61560]{1,0:T(8,128)} %convolution_bitcast_fusion) | data formatting | bytes 13296960 | tf_op jit(solution)/shard_map/reshape | solution.py:73
  501.6 25.2 %stack.11 = f32[27,61560]{1,0:T(8,128)} concatenate(f32[1,61560]{1,0:T(1,128)} %stack_reshape.297, f32[1,61560]{1,0:T(1,128)} %stack_reshape.298, f32[1,61560]{1,0:T(1,128)} %stack_reshape.299, f32[1,61560]{1,0:T(1,128)} %stack_reshape.300, f32[1,61560]{1,0:T(1,128)} %stack_reshape.301, f32[1,61560]{1,0:T(1,128)} %stack_reshape.302, f32[1,61560]{1,0:T(1,128)} %stack_reshape.303, ...), dimensions={0} | concatenate | bytes 13296960 | tf_op jit(solution)/shard_map/stack | solution.py:214
  526.8 11.2 %fusion.42 = f32[32,27]{1,0:T(8,128)} fusion(f32[32,61560]{1,0:T(8,128)} %reshape.118, f32[27,61560]{1,0:T(8,128)} %stack.11), kind=kOutput, calls=%fused_computation.162 | convolution fusion | flops 638254080 | bytes 14531616 | tf_op jit(solution)/shard_map/dot_general | solution.py:216
  547.5 9.7 %stack.10 = f32[27,32768]{1,0:T(8,128)} concatenate(f32[1,32768]{1,0:T(1,128)S(1)} %stack_reshape.270, f32[1,32768]{1,0:T(1,128)S(1)} %stack_reshape.271, f32[1,32768]{1,0:T(1,128)S(1)} %stack_reshape.272, f32[1,32768]{1,0:T(1,128)S(1)} %stack_reshape.273, f32[1,32768]{1,0:T(1,128)S(1)} %stack_reshape.274, f32[1,32768]{1,0:T(1,128)S(1)} %stack_reshape.275, ...), dimensions={0} | concatenate | bytes 7077888 | tf_op jit(solution)/shard_map/stack | solution.py:213
  568.4 17.3 %all-reduce.6 = (f32[]{:T(128)}, f32[32,27]{1,0:T(8,128)S(1)}, f32[32]{0:T(128)S(1)}, f32[32,27]{1,0:T(8,128)S(1)}, f32[1]{0:T(128)}) all-reduce(f32[]{:T(128)S(6)} %div.17, f32[32,27]{1,0:T(8,128)S(1)} %fusion.41, ...), channel_id=1, replica_groups=mesh['subset_0'=4,'subset_1'=2,'subset_2'=2,'slab_0'=4,'slab_1'=4] {'sub..., use_global_device_ids=true, to_apply=%region_5.6 | all-reduce | flops 1762 | bytes 14096 | tf_op jit(solution)/shard_map/psum | solution.py:49
  585.7 11.3 %all-reduce.8 = (f32[]{:T(128)}, f32[32,27]{1,0:T(8,128)S(1)}, f32[32]{0:T(128)S(1)}, f32[32,27]{1,0:T(8,128)S(1)}, f32[1]{0:T(128)}) all-reduce(f32[]{:T(128)} %get-tuple-element.244, f32[32,27]{1,0:T(8,128)S(1)} %get-tuple-element.245, ...), channel_id=1, replica_groups=mesh['subset_0'=4,'subset_1'=2,'subset_2'=2,'slab_0'=4,'slab_1'=4] {'sub..., use_global_device_ids=true, to_apply=%region_6.7 | all-reduce | flops 1762 | bytes 14096 | tf_op jit(solution)/shard_map/psum | solution.py:49
  601.5 15.7 %all-reduce.5 = (f32[]{:T(128)}, f32[32,27]{1,0:T(8,128)S(1)}, f32[32]{0:T(128)S(1)}, f32[32,27]{1,0:T(8,128)S(1)}, f32[1]{0:T(128)}) all-reduce(f32[]{:T(128)} %get-tuple-element.249, f32[32,27]{1,0:T(8,128)S(1)} %get-tuple-element.250, ...), channel_id=1, replica_groups=mesh['subset_0'=4,'subset_1'=2,'subset_2'=2,'slab_0'=4,'slab_1'=4] {'sla..., use_global_device_ids=true, to_apply=%region_8.9 | all-reduce | flops 1762 | bytes 14096 | tf_op jit(solution)/shard_map/psum | solution.py:49
  617.2 19.5 %all-reduce.4 = (f32[]{:T(128)}, f32[32,27]{1,0:T(8,128)}, f32[32]{0:T(128)}, f32[32,27]{1,0:T(8,128)}, f32[1]{0:T(128)}) all-reduce(f32[]{:T(128)} %get-tuple-element.239, f32[32,27]{1,0:T(8,128)S(1)} %get-tuple-element.240, ...), channel_id=1, replica_groups=mesh['subset_0'=4,'subset_1'=2,'subset_2'=2,'slab_0'=4,'slab_1'=4] {'sla..., use_global_device_ids=true, to_apply=%region_9.10 | all-reduce | flops 1762 | bytes 14096 | tf_op jit(solution)/shard_map/psum | solution.py:49
  (226 shorter events, 202.7 us)
Async XLA Ops:
  7.2 412.1 %copy-start = (f32[32,27]{1,0:T(8,128)S(1)}, f32[32,27]{1,0:T(8,128)}, u32[]{:S(2)}) copy-start(f32[32,27]{1,0:T(8,128)} %param.12) | copy-start | bytes 10372
  7.2 243.7 %reduce-scatter.2.cloned.1.call-start = ((), (), s32[]{:S(2)}) async-start(), calls=%async_computation.2 | async-start | bytes 4456448 | tf_op jit(solution)/shard_map/reduce_scatter | solution.py:160
  254.3 186.4 %all-to-all-start = ((f32[16,2,4,8,1024]{4,3,2,1,0:T(8,128)}), f32[16,2,4,8,1024]{4,3,2,1,0:T(8,128)}, u32[]{:S(2)}, u32[]{:S(2)}) async-start(f32[16,2,4,8,1024]{4,3,2,1,0:T(8,128)} %broadcast_in_dim.45), calls=%async_computation.1 | async-start | bytes 8388608 | tf_op jit(solution)/shard_map/all_to_all | solution.py:26
  260.4 1.4 collective-permute-start
  261.9 8.2 %collective-permute-start.1 = (f32[1,8,1024]{2,1,0:T(8,128)S(1)}, f32[1,8,1024]{2,1,0:T(8,128)S(1)}, u32[]{:S(2)}, u32[]{:S(2)}) collective-permute-start(f32[1,8,1024]{2,1,0:T(8,128)S(1)} %get-tuple-element.350), channel_id=1, source_target_pairs={{0,1},{1,2},{2,3},{3,4},{4,5},{5,6},{6,7},{7,8},{8,9},{9,10},{10,1... | collective-permute-start | bytes 98312 | tf_op jit(solution)/shard_map/ppermute | solution.py:42
  263.7 47.0 %collective-permute-start.2 = (f32[1,8,1024]{2,1,0:T(8,128)S(1)}, f32[1,8,1024]{2,1,0:T(8,128)S(1)}, u32[]{:S(2)}, u32[]{:S(2)}) collective-permute-start(f32[1,8,1024]{2,1,0:T(8,128)S(1)} %get-tuple-element.351), channel_id=1, source_target_pairs={{1,0},{2,1},{3,2},{4,3},{5,4},{6,5},{7,6},{8,7},{9,8},{10,9},{11,1... | collective-permute-start | bytes 98312 | tf_op jit(solution)/shard_map/ppermute | solution.py:43
  310.7 1.4 collective-permute-start.3
  318.5 14.0 %copy-start.14 = (f32[32,27]{1,0:T(8,128)S(1)}, f32[32,27]{1,0:T(8,128)}, u32[]{:S(2)}) copy-start(f32[32,27]{1,0:T(8,128)} %param.10) | copy-start | bytes 10372
  318.5 14.0 %copy-start.15 = (f32[32]{0:T(128)S(1)}, f32[32]{0:T(128)}, u32[]{:S(2)}) copy-start(f32[32]{0:T(128)} %param.11) | copy-start | bytes 388
  343.2 44.3 %collective-permute-start.4 = (f32[32,1,8,1024]{3,2,1,0:T(8,128)S(1)}, f32[32,1,8,1024]{3,2,1,0:T(8,128)S(1)}, u32[]{:S(2)}, u32[]{:S(2)}) collective-permute-start(f32[32,1,8,1024]{3,2,1,0:T(8,128)S(1)} %get-tuple-element.263), channel_id=1, source_target_pairs={{0,1},{1,2},{2,3},{3,4},{4,5},{5,6},{6,7},{7,8},{8,9},{9,10},{10,1... | collective-permute-start | bytes 3145736 | tf_op jit(solution)/shard_map/ppermute | solution.py:42
  345.3 48.6 %collective-permute-start.5 = (f32[32,1,8,1024]{3,2,1,0:T(8,128)S(1)}, f32[32,1,8,1024]{3,2,1,0:T(8,128)S(1)}, u32[]{:S(2)}, u32[]{:S(2)}) collective-permute-start(f32[32,1,8,1024]{3,2,1,0:T(8,128)S(1)} %get-tuple-element.264), channel_id=1, source_target_pairs={{1,0},{2,1},{3,2},{4,3},{5,4},{6,5},{7,6},{8,7},{9,8},{10,9},{11,1... | collective-permute-start | bytes 3145736 | tf_op jit(solution)/shard_map/ppermute | solution.py:43
  394.2 4.7 collective-permute-start.6
  454.5 83.5 %collective-permute-start.7 = (f32[1,8,1024]{2,1,0:T(8,128)}, f32[1,8,1024]{2,1,0:T(8,128)S(1)}, u32[]{:S(2)}, u32[]{:S(2)}) collective-permute-start(f32[1,8,1024]{2,1,0:T(8,128)} %get-tuple-element.348), channel_id=1, source_target_pairs={{0,1},{1,2},{2,3},{3,4},{4,5},{5,6},{6,7},{7,8},{8,9},{9,10},{10,1... | collective-permute-start | bytes 98312 | tf_op jit(solution)/shard_map/ppermute | solution.py:42
  454.5 83.5 %collective-permute-start.8 = (f32[1,8,1024]{2,1,0:T(8,128)}, f32[1,8,1024]{2,1,0:T(8,128)}, u32[]{:S(2)}, u32[]{:S(2)}) collective-permute-start(f32[1,8,1024]{2,1,0:T(8,128)} %get-tuple-element.349), channel_id=1, source_target_pairs={{1,0},{2,1},{3,2},{4,3},{5,4},{6,5},{7,6},{8,7},{9,8},{10,9},{11,1... | collective-permute-start | bytes 98312 | tf_op jit(solution)/shard_map/ppermute | solution.py:43
  470.9 26.1 %copy-start.8 = (f32[6,10,1026]{2,1,0:T(8,128)S(1)}, f32[6,10,1026]{2,1,0:T(8,128)}, u32[]{:S(2)}) copy-start(f32[6,10,1026]{2,1,0:T(8,128)} %get-tuple-element.333) | copy-start | bytes 738724
  473.0 25.0 %copy-start.7 = (f32[6,10,1026]{2,1,0:T(8,128)S(1)}, f32[6,10,1026]{2,1,0:T(8,128)}, u32[]{:S(2)}) copy-start(f32[6,10,1026]{2,1,0:T(8,128)} %get-tuple-element.334) | copy-start | bytes 738724
  475.2 23.9 %copy-start.6 = (f32[6,10,1026]{2,1,0:T(8,128)S(1)}, f32[6,10,1026]{2,1,0:T(8,128)}, u32[]{:S(2)}) copy-start(f32[6,10,1026]{2,1,0:T(8,128)} %get-tuple-element.335) | copy-start | bytes 738724
  477.4 22.2 %copy-start.5 = (f32[6,10,1026]{2,1,0:T(8,128)S(1)}, f32[6,10,1026]{2,1,0:T(8,128)}, u32[]{:S(2)}) copy-start(f32[6,10,1026]{2,1,0:T(8,128)} %get-tuple-element.336) | copy-start | bytes 738724
  479.6 20.4 %copy-start.4 = (f32[6,10,1026]{2,1,0:T(8,128)S(1)}, f32[6,10,1026]{2,1,0:T(8,128)}, u32[]{:S(2)}) copy-start(f32[6,10,1026]{2,1,0:T(8,128)} %get-tuple-element.337) | copy-start | bytes 738724
  481.8 18.7 %copy-start.3 = (f32[6,10,1026]{2,1,0:T(8,128)S(1)}, f32[6,10,1026]{2,1,0:T(8,128)}, u32[]{:S(2)}) copy-start(f32[6,10,1026]{2,1,0:T(8,128)} %get-tuple-element.338) | copy-start | bytes 738724
  484.0 16.9 %copy-start.2 = (f32[6,10,1026]{2,1,0:T(8,128)S(1)}, f32[6,10,1026]{2,1,0:T(8,128)}, u32[]{:S(2)}) copy-start(f32[6,10,1026]{2,1,0:T(8,128)} %get-tuple-element.339) | copy-start | bytes 738724
  526.8 12.0 %copy-start.11 = (f32[4,8,1024]{2,1,0:T(8,128)S(1)}, f32[4,8,1024]{2,1,0:T(8,128)}, u32[]{:S(2)}) copy-start(f32[4,8,1024]{2,1,0:T(8,128)} %get-tuple-element.261) | copy-start | bytes 393220
  526.8 12.0 %copy-start.12 = (f32[4,8,1024]{2,1,0:T(8,128)S(1)}, f32[4,8,1024]{2,1,0:T(8,128)}, u32[]{:S(2)}) copy-start(f32[4,8,1024]{2,1,0:T(8,128)} %get-tuple-element.262) | copy-start | bytes 393220
  538.8 1.3 collective-permute-start.9
  (4 other events, 20.8 us)
Sparse Core Ops, SparseCore 0:
  153.3 97.5 reduce-scatter.1
where the time goes:
time: 656 us; the launch traced here: 644 us
  local copies, waits for them, and re-layouts  264 us (40%)
  waiting for transfers between devices  191 us (29%)
  blocking collectives  68.3 us (10%)
  matrix products  65.5 us (10%)
  starting transfers between devices  26.6 us (4%)
  between operations  16.3 us (2%)
  other arithmetic  11.9 us (2%)
    reduce_scatter x1, waiting for transfers between devices, body(): lax.psum_scatter(backproject(sino_order, angles, local_views), SLAB, scat...  97.7 us
    dynamic_update_slice x16, local copies, waits for them, and re-layouts, one_row(): lax.dynamic_update_slice(inner, previous + part_row[:, None, :], start_at)  90.7 us
    psum x5, blocking collectives, one_axis_at_a_time(): return functools.reduce(lax.psum, axes, value)  68.3 us
    another operation x28, local copies, waits for them, and re-layouts, body(): wide_patches = jnp.stack(wide_pieces)  65.2 us
    ppermute x3, waiting for transfers between devices, extended_2(): after = lax.ppermute(initial, axis, down)  47.1 us
    ppermute x3, waiting for transfers between devices, extended_2(): before = lax.ppermute(last, axis, up)  39.8 us
    dynamic_slice x16, local copies, waits for them, and re-layouts, one_row(): previous = lax.dynamic_slice(inner, start_at, (count_rows, 1, X))  24.8 us
    dot_general x8, matrix products, one_row(): lax.dot_general(sino, weights, (((0, 2), (0, 2)), ((), ())), preferred_el...  23.9 us
  transfers between devices with their start and end apart: 12, of which 8 were waited for; matrix products, arithmetic and copies ran while one was open for 23% of the time, Pallas kernels for 0%

commit v1 on v0

v1 whole, which is shorter than its diff:
```python
import math

import jax
import jax.numpy as jnp
from jax import lax
from jax.experimental import pallas as pl
from jax.experimental.pallas import tpu as pltpu
from jax.sharding import Mesh
from jax.sharding import PartitionSpec as P

DET = 2048
X = 1024
Y = 8
DEPTH = 4
SUBS = 8
SLABS = 16
GROUP = 2 * SLABS
VPS = 64
FIRST_COL = 384
COLS = 1280
PATCH = 80
CELLS = float(SUBS * 128 * Y * X)
MESH = pl.DeviceIdType.MESH
F32 = jnp.float32
BF16 = jnp.bfloat16

GATHER = lax.GatherDimensionNumbers(
    offset_dims=(),
    collapsed_slice_dims=(1,),
    start_index_map=(1,),
    operand_batching_dims=(0,),
    start_indices_batching_dims=(0,),
)


def iota(shape, dim):
    return lax.broadcasted_iota(jnp.int32, shape, dim)


def exact_dot(a, b):
    return jnp.dot(a, b, precision=lax.Precision.HIGHEST, preferred_element_type=F32)


def dot_nt(a, b, precision=None):
    return lax.dot_general(
        a, b, (((1,), (1,)), ((), ())), precision=precision, preferred_element_type=F32
    )


def split(value):
    high = value.astype(BF16)
    return high, (value - high.astype(F32)).astype(BF16)


def tap_of(column, shift_y):
    block = column >> 3
    shift_z = (block >= 3).astype(jnp.int32) + (block >= 6).astype(jnp.int32)
    return 6 * shift_z + block + 3 * shift_y


def build_first(w_first, b_first):
    pick = (iota((256, 32), 0) >> 3 == iota((256, 32), 1)).astype(F32)
    rows = exact_dot(pick, w_first)
    bias = jnp.sum(pick * b_first, axis=1, keepdims=True)
    row, col = iota((256, PATCH), 0), iota((256, PATCH), 1)
    out = jnp.where(col == 72, bias, 0.0)
    for shift_y in range(3):
        expand = iota((27, PATCH), 0) == tap_of(iota((27, PATCH), 1), shift_y)
        expand = (expand & (iota((27, PATCH), 1) < 72)).astype(F32)
        near = (col & 7) - (row & 7) == shift_y - 1
        out = out + jnp.where(near & (col < 72), exact_dot(rows, expand), 0.0)
    high, low = split(out)
    return jnp.concatenate([high, low, high], axis=1)


def build_second(w_second):
    pick = (iota((256, 32), 0) >> 3 == iota((256, 32), 1)).astype(F32)
    rows = exact_dot(pick, w_second)
    row, col = iota((256, PATCH), 0), iota((256, PATCH), 1)
    pick_t = (iota((32, 256), 1) >> 3 == iota((32, 256), 0)).astype(F32)
    row_t, col_t = iota((PATCH, 256), 0), iota((PATCH, 256), 1)
    out = jnp.zeros((256, PATCH), F32)
    out_t = jnp.zeros((PATCH, 256), F32)
    for shift_y in range(3):
        expand = iota((27, PATCH), 0) == tap_of(iota((27, PATCH), 1), shift_y)
        expand = (expand & (iota((27, PATCH), 1) < 72)).astype(F32)
        near = (row & 7) - (col & 7) == shift_y - 1
        out = out + jnp.where(near & (col < 72), exact_dot(rows, expand), 0.0)
        expand_t = iota((PATCH, 27), 1) == tap_of(iota((PATCH, 27), 0), shift_y)
        expand_t = (expand_t & (iota((PATCH, 27), 0) < 72)).astype(F32)
        taps_t = dot_nt(expand_t, w_second, lax.Precision.HIGHEST)
        near_t = (col_t & 7) - (row_t & 7) == shift_y - 1
        out_t = out_t + jnp.where(near_t & (row_t < 72), exact_dot(taps_t, pick_t), 0.0)
    high, low = split(out)
    return jnp.concatenate([high, low, high], axis=1), jnp.concatenate(split(out_t), axis=0)


def gather_grads(first, second):
    pick_t = (iota((32, 256), 1) >> 3 == iota((32, 256), 0)).astype(F32)
    row, col = iota((256, PATCH), 0), iota((256, PATCH), 1)
    frow, fcol = iota((PATCH, 128), 0), iota((PATCH, 128), 1)
    out = jnp.zeros((32, 128), F32)
    for shift_y in range(3):
        near = ((col & 7) - (row & 7) == shift_y - 1) & (col < 72)
        to = (fcol == tap_of(frow, shift_y)) & (frow < 72)
        if shift_y == 1:
            near = near | (col == 72)
            to = to | ((frow == 72) & (fcol == 27))
        out = out + exact_dot(exact_dot(pick_t, jnp.where(near, first, 0.0)), to.astype(F32))
        near = ((row & 7) - (col & 7) == shift_y - 1) & (col < 72)
        to = (fcol == tap_of(frow, shift_y) + 32) & (frow < 72)
        out = out + exact_dot(exact_dot(pick_t, jnp.where(near, second, 0.0)), to.astype(F32))
    return out


def shifted(value, by):
    lane = iota(value.shape, 1)
    if by == 1:
        return jnp.where(lane == 0, 0.0, pltpu.roll(value, 1, 1))
    return jnp.where(lane == X - 1, 0.0, pltpu.roll(value, X - 1, 1))


def exchange_kernel(
    sino,
    table,
    w_first,
    b_first,
    w_second,
    recv,
    tables,
    first_cat,
    second_cat,
    second_t,
    send,
    send_sem,
    recv_sem,
    tsend_sem,
    trecv_sem,
):
    sub, half, slab = lax.axis_index("sub"), lax.axis_index("half"), lax.axis_index("slab")
    me = half * SLABS + slab

    def peer(other):
        return (sub, other // SLABS, lax.rem(other, SLABS))

    def signal(p, carry):
        other = lax.rem(me + p, GROUP)
        pl.semaphore_signal(
            pltpu.get_barrier_semaphore(), inc=1, device_id=peer(other), device_id_type=MESH
        )
        return carry

    lax.fori_loop(1, GROUP, signal, 0)

    def pack(q, carry):
        at = pl.multiple_of(q * 16, 16)
        zero = sino[0, pl.ds(at, 16), FIRST_COL : FIRST_COL + COLS].astype(F32)
        one = sino[1, pl.ds(at, 16), FIRST_COL : FIRST_COL + COLS].astype(F32)
        for i in range(4):
            rows = jnp.concatenate([zero[4 * i : 4 * i + 4], one[4 * i : 4 * i + 4]], axis=0)
            send[4 * q + i] = jnp.concatenate(
                [rows[:, : COLS // 2], rows[:, COLS // 2 :]], axis=0
            ).astype(BF16)
        return carry

    lax.fori_loop(0, GROUP // 4, pack, 0)
    recv[me] = send[me]
    tables[me] = table[...]
    pl.semaphore_wait(pltpu.get_barrier_semaphore(), GROUP - 1)

    def copies(p):
        other = lax.rem(me + p, GROUP)
        data = pltpu.make_async_remote_copy(
            src_ref=send.at[other],
            dst_ref=recv.at[me],
            send_sem=send_sem.at[other],
            recv_sem=recv_sem.at[me],
            device_id=peer(other),
            device_id_type=MESH,
        )
        small = pltpu.make_async_remote_copy(
            src_ref=table,
            dst_ref=tables.at[me],
            send_sem=tsend_sem.at[other],
            recv_sem=trecv_sem.at[me],
            device_id=peer(other),
            device_id_type=MESH,
        )
        return data, small

    def arrivals(p):
        other = lax.rem(me + p, GROUP)
        data = pltpu.make_async_remote_copy(
            src_ref=send.at[other],
            dst_ref=recv.at[other],
            send_sem=send_sem.at[other],
            recv_sem=recv_sem.at[other],
            device_id=peer(other),
            device_id_type=MESH,
        )
        small = pltpu.make_async_remote_copy(
            src_ref=table,
            dst_ref=tables.at[other],
            send_sem=tsend_sem.at[other],
            recv_sem=trecv_sem.at[other],
            device_id=peer(other),
            device_id_type=MESH,
        )
        return data, small

    def start(p, carry):
        for copy in copies(p):
            copy.start()
        return carry

    lax.fori_loop(1, GROUP, start, 0)
    first_cat[...] = build_first(w_first[...], b_first[...])
    second_cat[...], second_t[...] = build_second(w_second[...])

    def finish(p, carry):
        for copy in arrivals(p):
            copy.wait()
        return carry

    lax.fori_loop(1, GROUP, finish, 0)


def take(source, index):
    return lax.gather(
        source, index[..., None], GATHER, (1, 1), mode=lax.GatherScatterMode.PROMISE_IN_BOUNDS
    )


def backproject_kernel(table, recv, out, rows):
    def widen(s, carry):
        block = recv[s].astype(F32)
        row = jnp.concatenate([block[:8], block[8:]], axis=1)
        rows[0, s] = row
        rows[1, s] = pltpu.roll(row, COLS - 64, 1)
        return carry

    lax.fori_loop(0, GROUP, widen, 0)
    row_pos = iota((8, 128), 0).astype(F32) - (Y - 1) / 2.0
    lane = iota((8, 128), 1).astype(F32)
    out[...] = jnp.zeros_like(out)

    def one_sender(s, carry):
        for block in range(X // 128):
            here = slice(block * 128, (block + 1) * 128)
            total = [out[z, :, here] for z in range(DEPTH)]
            for v in range(2):
                cosine, sine = table[s, 2 * v], table[s, 2 * v + 1]
                step = table[s, 4 + v * 8 + block].astype(jnp.int32)
                pos = (
                    (lane + (128.0 * block - (X - 1) / 2.0)) * cosine + row_pos * sine
                ) + (DET - 1) / 2.0
                lower = jnp.floor(pos)
                part = pos - lower
                w_high = part.astype(BF16).astype(F32)
                w_low = (1.0 - part).astype(BF16).astype(F32)
                index = lower.astype(jnp.int32) - (FIRST_COL + 64 * step)
                index = jnp.concatenate([index, index], axis=0)
                at_low = (index & 127).astype(jnp.int16)
                at_high = ((index + 1) & 127).astype(jnp.int16)
                whole = index.astype(jnp.int16)
                in_low = whole < jnp.int16(128)
                in_high = whole < jnp.int16(127)
                copy = step & 1
                at = pl.multiple_of((step >> 1) * 128, 128)
                for pair in range(2):

                    def source(offset):
                        parts = [
                            jnp.broadcast_to(
                                rows[
                                    copy, s, pl.ds(v * 4 + 2 * pair + q, 1), pl.ds(at + offset, 128)
                                ],
                                (8, 128),
                            )
                            for q in range(2)
                        ]
                        return jnp.concatenate(parts, axis=0).astype(BF16)

                    near, far = source(0), source(128)
                    low = jnp.where(in_low, take(near, at_low), take(far, at_low)).astype(F32)
                    high = jnp.where(in_high, take(near, at_high), take(far, at_high)).astype(F32)
                    for q in range(2):
                        z = 2 * pair + q
                        half = slice(8 * q, 8 * q + 8)
                        total[z] = total[z] + (w_low * low[half] + w_high * high[half])
            for z in range(DEPTH):
                out[z, :, here] = total[z]
        return carry

    lax.fori_loop(0, GROUP, one_sender, 0)
    out[...] = out[...] * (math.pi / VPS)


def network_kernel(
    own,
    first_cat,
    second_cat,
    second_t,
    b_second,
    pred_out,
    target_out,
    grads_out,
    field,
    totals,
    near_u,
    patch_u,
    hidden_all,
    taps,
    near_r,
    acc_first,
    acc_second,
    part_slots,
    whole_slots,
    mine,
    halo_send,
    halo_recv,
    tot_send,
    tot_recv,
    slab_send,
    slab_recv,
    sub_send,
    sub_recv,
):
    sub, half, slab = lax.axis_index("sub"), lax.axis_index("half"), lax.axis_index("slab")
    me = half * SLABS + slab
    pair = sub * 2 + half

    def ring(other):
        return (sub, other // SLABS, lax.rem(other, SLABS))

    before = ring(lax.rem(me + GROUP - 1, GROUP))
    after = ring(lax.rem(me + 1, GROUP))

    def slab_peer(p):
        other = lax.rem(slab + p, SLABS)
        return other, (sub, half, other)

    def pair_peer(p):
        other = lax.rem(pair + p, 2 * SUBS)
        return other, (other // 2, lax.rem(other, 2), slab)

    def sub_peer(p):
        other = lax.rem(sub + p, SUBS)
        return other, (other, half, slab)

    barrier = pltpu.get_barrier_semaphore()
    for target in (before, after):
        pl.semaphore_signal(barrier, inc=1, device_id=target, device_id_type=MESH)

    def greet(p, carry):
        for peer in (slab_peer, pair_peer):
            pl.semaphore_signal(
                pltpu.get_barrier_semaphore(), inc=1, device_id=peer(p)[1], device_id_type=MESH
            )
        return carry

    lax.fori_loop(1, 16, greet, 0)
    pl.semaphore_wait(barrier, 32)

    to_after = pltpu.make_async_remote_copy(
        src_ref=own.at[2:4],
        dst_ref=field.at[0:2],
        send_sem=halo_send.at[0],
        recv_sem=halo_recv.at[0],
        device_id=after,
        device_id_type=MESH,
    )
    to_before = pltpu.make_async_remote_copy(
        src_ref=own.at[0:2],
        dst_ref=field.at[6:8],
        send_sem=halo_send.at[1],
        recv_sem=halo_recv.at[1],
        device_id=before,
        device_id_type=MESH,
    )
    to_after.start()
    to_before.start()

    def total_copy(p, slot):
        other, target = sub_peer(p)
        return pltpu.make_async_remote_copy(
            src_ref=own,
            dst_ref=totals.at[sub if slot is None else other],
            send_sem=tot_send.at[other],
            recv_sem=tot_recv.at[sub if slot is None else other],
            device_id=target,
            device_id_type=MESH,
        )

    def send_total(p, carry):
        total_copy(p, None).start()
        return carry

    lax.fori_loop(1, SUBS, send_total, 0)
    field[2:6] = own[...]
    totals[sub] = own[...]
    taps[...] = jnp.zeros_like(taps)
    near_r[...] = jnp.zeros_like(near_r)
    acc_first[...] = jnp.zeros_like(acc_first)
    acc_second[...] = jnp.zeros_like(acc_second)
    to_after.wait()
    to_before.wait()

    for m in range(8):
        value = field[m]
        if m < 2:
            value = jnp.where(me > 0, value, 0.0)
        if m >= 6:
            value = jnp.where(me < GROUP - 1, value, 0.0)
        near_u[m] = jnp.concatenate([shifted(value, 1), value, shifted(value, -1)], axis=0)

    ones = (iota((8, X), 0) == 0).astype(F32)

    def forward(j, carry):
        patch = jnp.concatenate([near_u[j], near_u[j + 1], near_u[j + 2], ones], axis=0)
        high, low = split(patch)
        patch_u[j] = high
        pre = jnp.dot(
            first_cat[...], jnp.concatenate([high, high, low], axis=0), preferred_element_type=F32
        )
        outside = ((j == 0) & (me == 0)) | ((j == 5) & (me == GROUP - 1))
        hidden = jnp.maximum(pre, 0.0) * jnp.where(outside, 0.0, 1.0)
        high, low = split(hidden)
        hidden_all[j] = high
        main = jnp.dot(second_t[...], high, preferred_element_type=F32)
        rest = jnp.dot(second_t[0:PATCH], low, preferred_element_type=F32)
        added = main[:72] + (main[PATCH : PATCH + 72] + rest[:72])
        for shift_z in range(3):
            at = j - shift_z + 2
            taps[at] = taps[at] + added[24 * shift_z : 24 * shift_z + 24]
        return carry

    lax.fori_loop(0, 6, forward, 0)

    def finish_total(p, carry):
        total_copy(p, 1).wait()
        return carry

    lax.fori_loop(1, SUBS, finish_total, 0)

    sum_square = jnp.zeros((8, X), F32)
    sum_resid = jnp.zeros((8, X), F32)
    for i in range(DEPTH):
        value = own[i]
        conv = shifted(taps[i + 2, 0:8], 1) + taps[i + 2, 8:16] + shifted(taps[i + 2, 16:24], -1)
        pred = value + conv + b_second[0]
        total = totals[0, i]
        for s in range(1, SUBS):
            total = total + totals[s, i]
        target = (total - value) / (SUBS - 1)
        pred_out[i] = pred
        target_out[i] = target
        diff = pred - target
        resid = (2.0 * diff) / CELLS
        sum_square = sum_square + diff * diff
        sum_resid = sum_resid + resid
        near_r[i + 2] = jnp.concatenate([shifted(resid, -1), resid, shifted(resid, 1)], axis=0)

    nothing = jnp.zeros((8, X), F32)

    def backward(j, carry):
        patch = jnp.concatenate([near_r[j + 2], near_r[j + 1], near_r[j], nothing], axis=0)
        high, low = split(patch)
        grad = jnp.dot(
            second_cat[...], jnp.concatenate([high, high, low], axis=0), preferred_element_type=F32
        )
        hidden = hidden_all[j]
        acc_second[...] += dot_nt(hidden, high)
        grad = jnp.where(hidden.astype(F32) > 0.0, grad, 0.0).astype(BF16)
        acc_first[...] += dot_nt(grad, patch_u[j])
        return carry

    lax.fori_loop(0, 6, backward, 0)

    packed = gather_grads(acc_first[...], acc_second[...])
    row, lane = iota((32, 128), 0), iota((32, 128), 1)
    packed = packed + jnp.where(
        (row == 0) & (lane == 64), jnp.sum(sum_square) / CELLS, 0.0
    )
    packed = packed + jnp.where((row == 0) & (lane == 65), jnp.sum(sum_resid), 0.0)

    mine[0] = packed
    part_slots[slab] = packed

    def slab_copy(p, arriving):
        other, target = slab_peer(p)
        slot = other if arriving else slab
        return pltpu.make_async_remote_copy(
            src_ref=mine.at[0],
            dst_ref=part_slots.at[slot],
            send_sem=slab_send.at[other],
            recv_sem=slab_recv.at[slot],
            device_id=target,
            device_id_type=MESH,
        )

    def pair_copy(p, arriving):
        other, target = pair_peer(p)
        slot = other if arriving else pair
        return pltpu.make_async_remote_copy(
            src_ref=mine.at[1],
            dst_ref=whole_slots.at[slot],
            send_sem=sub_send.at[other],
            recv_sem=sub_recv.at[slot],
            device_id=target,
            device_id_type=MESH,
        )

    def started(make):
        def step(p, carry):
            make(p, False).start()
            return carry

        lax.fori_loop(1, 16, step, 0)

    def finished(make):
        def step(p, carry):
            make(p, True).wait()
            return carry

        lax.fori_loop(1, 16, step, 0)

    started(slab_copy)
    finished(slab_copy)
    packed = part_slots[0]
    for s in range(1, 16):
        packed = packed + part_slots[s]
    mine[1] = packed
    whole_slots[pair] = packed
    started(pair_copy)
    finished(pair_copy)
    packed = whole_slots[0]
    for s in range(1, 16):
        packed = packed + whole_slots[s]
    grads_out[...] = packed


def view_table(angles):
    cosine, sine = jnp.cos(angles), jnp.sin(angles)
    first = jnp.arange(X // 128, dtype=F32) * 128.0 - (X - 1) / 2.0
    ends = jnp.minimum(first * cosine[:, None], (first + 127.0) * cosine[:, None])
    least = ends - 3.5 * jnp.abs(sine)[:, None] + (DET - 1) / 2.0
    step = jnp.floor((jnp.floor(least) - (FIRST_COL + 1.0)) / 64.0)
    line = jnp.concatenate(
        [jnp.stack([cosine, sine], axis=1).reshape(-1), step.reshape(-1), jnp.zeros(108, F32)]
    )
    return jnp.broadcast_to(line[None], (8, 128))


VMEM = pl.BlockSpec(memory_space=pltpu.VMEM)
SMEM = pl.BlockSpec(memory_space=pltpu.SMEM)


def shape(dims, dtype=F32):
    return jax.ShapeDtypeStruct(dims, dtype)


def body(sinogram, angles, w_first, b_first, w_second, b_second):
    dma = pltpu.SemaphoreType.DMA
    recv, tables, first_cat, second_cat, second_t = pl.pallas_call(
        exchange_kernel,
        name="exchange",
        out_shape=(
            shape((GROUP, 16, COLS // 2), BF16),
            shape((GROUP, 8, 128)),
            shape((256, 3 * PATCH), BF16),
            shape((256, 3 * PATCH), BF16),
            shape((2 * PATCH, 256), BF16),
        ),
        in_specs=[VMEM] * 5,
        out_specs=[VMEM] * 5,
        scratch_shapes=[
            pltpu.VMEM((GROUP, 16, COLS // 2), BF16),
            dma((GROUP,)),
            dma((GROUP,)),
            dma((GROUP,)),
            dma((GROUP,)),
        ],
        compiler_params=pltpu.CompilerParams(
            collective_id=0, has_side_effects=True, vmem_limit_bytes=32 << 20
        ),
    )(sinogram, view_table(angles), w_first, b_first[None], w_second)
    own = pl.pallas_call(
        backproject_kernel,
        name="backproject",
        out_shape=shape((DEPTH, Y, X)),
        in_specs=[SMEM, VMEM],
        out_specs=VMEM,
        scratch_shapes=[pltpu.VMEM((2, GROUP, 8, COLS), F32)],
        compiler_params=pltpu.CompilerParams(vmem_limit_bytes=32 << 20),
    )(tables[:, 0, :], recv)
    pred, target, grads = pl.pallas_call(
        network_kernel,
        name="network",
        out_shape=(shape((DEPTH, Y, X)), shape((DEPTH, Y, X)), shape((32, 128))),
        in_specs=[VMEM] * 4 + [SMEM],
        out_specs=[VMEM] * 3,
        scratch_shapes=[
            pltpu.VMEM((8, Y, X), F32),
            pltpu.VMEM((SUBS, DEPTH, Y, X), F32),
            pltpu.VMEM((8, 24, X), F32),
            pltpu.VMEM((6, PATCH, X), BF16),
            pltpu.VMEM((6, 256, X), BF16),
            pltpu.VMEM((8, 24, X), F32),
            pltpu.VMEM((8, 24, X), F32),
            pltpu.VMEM((256, PATCH), F32),
            pltpu.VMEM((256, PATCH), F32),
            pltpu.VMEM((16, 32, 128), F32),
            pltpu.VMEM((16, 32, 128), F32),
            pltpu.VMEM((2, 32, 128), F32),
            dma((2,)),
            dma((2,)),
            dma((SUBS,)),
            dma((SUBS,)),
            dma((16,)),
            dma((16,)),
            dma((16,)),
            dma((16,)),
        ],
        compiler_params=pltpu.CompilerParams(
            collective_id=1, has_side_effects=True, vmem_limit_bytes=48 << 20
        ),
    )(own, first_cat, second_cat, second_t, b_second)
    return (
        pred[None],
        target[None],
        grads[0, 64],
        grads[:, :27],
        grads[:, 27],
        grads[:, 32:59],
        grads[0, 65:66],
    )


def solution(mesh):
    finer = Mesh(mesh.devices.reshape(SUBS, 2, SLABS), ("sub", "half", "slab"))
    every = ("sub", "half", "slab")
    return jax.shard_map(
        body,
        mesh=finer,
        in_specs=(P(every, None, None), P(every), P(), P(), P(), P()),
        out_specs=(
            P(("sub", "half"), "slab", None, None),
            P(("sub", "half"), "slab", None, None),
            P(),
            P(),
            P(),
            P(),
            P(),
        ),
        check_vma=False,
    )
```

time: 656 us -> 96.3 us (0.15)
  the two profiles are of different devices: /device:TPU:32 before, /device:TPU:1 now
where the time goes in v1:
time: 96.3 us; the launch traced here: 96.1 us
  Pallas kernels  88.8 us (92%)
  local copies, waits for them, and re-layouts  5.76 us (6%)
  between operations  1.37 us (1%)
    pallas_call x1, Pallas kernels, body(): pl.pallas_call(network_kernel, name='network', out_shape=(shape((DEPTH, Y...  44.1 us
    pallas_call x1, Pallas kernels, body(): pl.pallas_call(exchange_kernel, name='exchange', out_shape=(shape((GROUP,...  29.4 us
    pallas_call x1, Pallas kernels, body(): pl.pallas_call(backproject_kernel, name='backproject', out_shape=shape((D...  15.3 us
    unnamed x10, local copies, waits for them, and re-layouts  2.8 us

profile of v1, /device:TPU:1, one launch (start us, length us, event | category | flops | bytes accessed | tf_op | source)
XLA Modules:
  0.0 96.1 jit_solution(2155318482933252533)
XLA Ops:
  0.6 0.7 fusion.4
  1.3 0.0 copy-start.3
  1.4 0.0 copy-start.1
  1.4 0.0 copy-start.2
  1.4 0.1 multiply_floor_fusion
  1.5 0.1 reshape.47
  1.6 0.1 copy.15
  1.7 0.1 reshape.41
  1.7 0.1 pad_maximum_fusion.1
  1.8 0.2 copy-done.3
  2.0 0.1 copy-done.1
  2.1 0.0 copy-done.2
  2.1 0.0 copy-start
  2.1 1.2 %copy-done = bf16[2,128,2048]{2,1,0:T(8,128)(2,1)S(1)} copy-done((bf16[2,128,2048]{2,1,0:T(8,128)(2,1)S(1)}, bf16[2,128,2048]{2,1,0:T(8,128)(2,1)}, u32[]{:S(2)}) %copy-start) | copy-done | bytes 1048600
  3.3 29.4 %exchange.1 = (bf16[32,16,640]{2,1,0:T(8,128)(2,1)S(1)}, f32[32,8,128]{2,1,0:T(8,128)S(1)}, bf16[256,240]{1,0:T(8,128)(2,1)S(1)}, bf16[256,240]{1,0:T(8,128)(2,1)S(1)}, bf16[160,256]{1,0:T(8,128)(2,1)S(1)}) custom-call(bf16[2,128,2048]{2,1,0:T(8,128)(2,1)S(1)} %copy-done, f32[8,128]{1,0:T(8,128)S(1)} %broadcast_in_dim.11.table, f32[32,27]{1,0:T(8,128)S(1)} %copy-done.1, ...), custom_call_target="tpu_custom_call" | custom-call | tf_op jit(solution)/shard_map/exchange/pallas_call | solution.py:565
  32.8 15.3 %backproject.1.own = f32[4,8,1024]{2,1,0:T(8,128)S(1)} custom-call(f32[32,128]{1,0:T(8,128)S(1)} %slice_bitcast_fusion.table, bf16[32,16,640]{2,1,0:T(8,128)(2,1)S(1)} %get-tuple-element.16.recv), custom_call_target="tpu_custom_call" | custom-call | tf_op jit(solution)/shard_map/backproject/pallas_call | solution.py:588
  48.7 44.1 %network.1 = (f32[4,8,1024]{2,1,0:T(8,128)S(1)}, f32[4,8,1024]{2,1,0:T(8,128)S(1)}, f32[32,128]{1,0:T(8,128)S(1)}) custom-call(f32[4,8,1024]{2,1,0:T(8,128)S(1)} %backproject.1.own, bf16[256,240]{1,0:T(8,128)(2,1)S(1)} %get-tuple-element.17.first_cat, bf16[256,240]{1,0:T(8,128)(2,1)S(1)} %get-tuple-element.18.second_cat, ...), custom_call_target="tpu_custom_call" | custom-call | tf_op jit(solution)/shard_map/network/pallas_call | solution.py:597
  92.8 0.7 fusion.3
  93.5 0.6 fusion.2
  94.1 0.7 slice_reduce_fusion
  94.8 0.7 copy.20
  95.5 0.7 copy.21
  (7 shorter events, 0.1 us)
Async XLA Ops:
  1.3 0.7 copy-start.3
  1.4 0.7 copy-start.1
  1.4 0.7 copy-start.2
  2.1 1.2 %copy-start = (bf16[2,128,2048]{2,1,0:T(8,128)(2,1)S(1)}, bf16[2,128,2048]{2,1,0:T(8,128)(2,1)}, u32[]{:S(2)}) copy-start(bf16[2,128,2048]{2,1,0:T(8,128)(2,1)} %sino.1) | copy-start | bytes 3145732

commit v2 on v1

v2 whole, which is shorter than its diff:
```python
import math

import jax
import jax.numpy as jnp
from jax import lax
from jax.experimental import pallas as pl
from jax.experimental.pallas import tpu as pltpu
from jax.sharding import Mesh
from jax.sharding import PartitionSpec as P

DET = 2048
X = 1024
Y = 8
CH = 32
DEPTH = 4
SUBS = 8
SLABS = 16
GROUP = 2 * SLABS
VPS = 64
FIRST_COL = 384
COLS = 1280
PATCH = 80
CELLS = float(SUBS * 128 * Y * X)
MESH = pl.DeviceIdType.MESH
F32 = jnp.float32
BF16 = jnp.bfloat16

GATHER = lax.GatherDimensionNumbers(
    offset_dims=(),
    collapsed_slice_dims=(1,),
    start_index_map=(1,),
    operand_batching_dims=(0,),
    start_indices_batching_dims=(0,),
)


def iota(shape, dim):
    return lax.broadcasted_iota(jnp.int32, shape, dim)


def exact_dot(a, b):
    return jnp.dot(a, b, precision=lax.Precision.HIGHEST, preferred_element_type=F32)


def dot_nt(a, b, precision=None):
    return lax.dot_general(
        a, b, (((1,), (1,)), ((), ())), precision=precision, preferred_element_type=F32
    )


def split(value):
    high = value.astype(BF16)
    return high, (value - high.astype(F32)).astype(BF16)


def tap_of(block, shift_y):
    shift_z = (block >= 3).astype(jnp.int32) + (block >= 6).astype(jnp.int32)
    return 6 * shift_z + block + 3 * shift_y


def build_first(w_first, b_first):
    pick = (iota((256, CH), 0) & (CH - 1) == iota((256, CH), 1)).astype(F32)
    rows = exact_dot(pick, w_first)
    bias = jnp.sum(pick * b_first, axis=1, keepdims=True)
    row, col = iota((256, PATCH), 0), iota((256, PATCH), 1)
    out = jnp.where(col == 72, bias, 0.0)
    tap, at = iota((27, PATCH), 0), iota((27, PATCH), 1)
    for shift_y in range(3):
        expand = ((tap == tap_of(at >> 3, shift_y)) & (at < 72)).astype(F32)
        near = (col & 7) - (row >> 5) == shift_y - 1
        out = out + jnp.where(near & (col < 72), exact_dot(rows, expand), 0.0)
    high, low = split(out)
    return jnp.concatenate([high, low, high], axis=1)


def build_second(w_second):
    pick = (iota((256, CH), 0) & (CH - 1) == iota((256, CH), 1)).astype(F32)
    rows = exact_dot(pick, w_second)
    row, col = iota((256, PATCH), 0), iota((256, PATCH), 1)
    pick_t = (iota((CH, 256), 1) & (CH - 1) == iota((CH, 256), 0)).astype(F32)
    row_t, col_t = iota((PATCH, 256), 0), iota((PATCH, 256), 1)
    out = jnp.zeros((256, PATCH), F32)
    out_t = jnp.zeros((PATCH, 256), F32)
    tap, at = iota((27, PATCH), 0), iota((27, PATCH), 1)
    tap_t, at_t = iota((PATCH, 27), 1), iota((PATCH, 27), 0)
    for shift_y in range(3):
        expand = ((tap == tap_of(at >> 3, shift_y)) & (at < 72)).astype(F32)
        near = (row >> 5) - (col & 7) == shift_y - 1
        out = out + jnp.where(near & (col < 72), exact_dot(rows, expand), 0.0)
        expand_t = ((tap_t == tap_of(at_t >> 3, shift_y)) & (at_t < 72)).astype(F32)
        taps_t = dot_nt(expand_t, w_second, lax.Precision.HIGHEST)
        near_t = (col_t >> 5) - (row_t & 7) == shift_y - 1
        out_t = out_t + jnp.where(near_t & (row_t < 72), exact_dot(taps_t, pick_t), 0.0)
    high, low = split(out)
    return jnp.concatenate([high, low, high], axis=1), jnp.concatenate(split(out_t), axis=0)


def build_gather():
    row, lane = iota((1024, 128), 0), iota((1024, 128), 1)
    y, col = row >> 7, row & 127
    block, near = col >> 3, col & 7
    shift = near - y + 1
    inside = (col < 72) & (shift >= 0) & (shift <= 2)
    first = (inside & (lane == tap_of(block, shift))) | ((col == 72) & (lane == 27))
    shift = y - near + 1
    inside = (col < 72) & (shift >= 0) & (shift <= 2)
    second = inside & (lane == tap_of(block, shift) + 32)
    return first.astype(F32).astype(BF16), second.astype(F32).astype(BF16)


def gathered(sums, gather):
    wide = jnp.concatenate([sums[CH * y : CH * y + CH] for y in range(Y)], axis=1)
    high, rest = wide.astype(BF16), wide
    rest = wide - high.astype(F32)
    middle, low = split(rest)
    out = jnp.dot(
        jnp.concatenate([high, middle, low], axis=0), gather, preferred_element_type=F32
    )
    return out[:CH] + (out[CH : 2 * CH] + out[2 * CH :])


def shifted(value, by):
    lane = iota(value.shape, 1)
    if by == 1:
        return jnp.where(lane == 0, 0.0, pltpu.roll(value, 1, 1))
    return jnp.where(lane == X - 1, 0.0, pltpu.roll(value, X - 1, 1))


def take(source, index):
    return lax.gather(
        source, index[..., None], GATHER, (1, 1), mode=lax.GatherScatterMode.PROMISE_IN_BOUNDS
    )


def view_pieces(angles):
    lane, row = iota((8, 128), 1), iota((8, 128), 0)
    angle = jnp.where(lane < 2, angles[0], angles[1])
    value = jnp.where(lane & 1 == 0, jnp.cos(angle), jnp.sin(angle))
    high = value.astype(BF16).astype(F32)
    middle = (value - high).astype(BF16).astype(F32)
    low = value - high - middle
    out = jnp.where(row == 0, high, jnp.where(row == 1, middle, jnp.where(row == 2, low, 0.0)))
    return jnp.where(lane < 4, out, 0.0)


def window_range(part_x):
    ends = (abs(128 * part_x - 511.5), abs(128 * part_x - 384.5))
    middle = (DET - 1) / 2.0
    first = (math.floor(middle - max(ends) - 4.0) - FIRST_COL - 1) // 64
    last = (math.floor(middle + min(ends) + 0.5) - FIRST_COL - 1) // 64
    return first, last


def add_sender(block, windows, out):
    value = block.astype(F32)
    row = jnp.concatenate([value[:8], value[8:]], axis=1)
    moved = pltpu.roll(row, COLS - 64, 1)
    tables = jnp.broadcast_to(value[0:1, :128] + value[1:2, :128] + value[2:3, :128], (8, 128))
    views = [take(tables, jnp.full((8, 128), i, jnp.int32)) for i in range(4)]
    row_index = iota((8, 128), 0)
    row_pos = row_index.astype(F32) - (Y - 1) / 2.0
    lane = iota((8, 128), 1).astype(F32)

    def piece(k):
        source = moved if k & 1 else row
        return source[:, (k >> 1) * 128 : (k >> 1) * 128 + 128]

    steps = []
    for part_x in range(X // 128):
        begin = 128.0 * part_x - (X - 1) / 2.0
        both = []
        for v in range(2):
            cosine, sine = views[2 * v], views[2 * v + 1]
            least = jnp.minimum(begin * cosine, (begin + 127.0) * cosine)
            least = (least - 3.5 * jnp.abs(sine)) + (DET - 1) / 2.0
            both.append(jnp.floor((jnp.floor(least) - (FIRST_COL + 1.0)) * (1.0 / 64.0)))
        steps.append(both)
        step = jnp.where(row_index < 4, both[0], both[1])
        first, last = window_range(part_x)
        near, far = piece(first), piece(first + 2)
        for k in range(first + 1, last + 1):
            reached = step >= float(k)
            near = jnp.where(reached, piece(k), near)
            far = jnp.where(reached, piece(k + 2), far)
        windows[part_x, :, :128] = near
        windows[part_x, :, 128:] = far
    for part_x in range(X // 128):
        here = slice(part_x * 128, (part_x + 1) * 128)
        total = [out[z, :, here] for z in range(DEPTH)]
        for v in range(2):
            cosine, sine = views[2 * v], views[2 * v + 1]
            pos = (
                (lane + (128.0 * part_x - (X - 1) / 2.0)) * cosine + row_pos * sine
            ) + (DET - 1) / 2.0
            lower = jnp.floor(pos)
            part = pos - lower
            w_high = part.astype(BF16).astype(F32)
            w_low = (1.0 - part).astype(BF16).astype(F32)
            index = (lower - (64.0 * steps[part_x][v] + FIRST_COL)).astype(jnp.int32)
            index = jnp.concatenate([index, index], axis=0)
            at_low = (index & 127).astype(jnp.int16)
            at_high = ((index + 1) & 127).astype(jnp.int16)
            whole = index.astype(jnp.int16)
            in_low = whole < jnp.int16(128)
            in_high = whole < jnp.int16(127)
            for pair in range(2):

                def source(offset):
                    parts = [
                        jnp.broadcast_to(
                            windows[part_x, pl.ds(v * 4 + 2 * pair + q, 1), pl.ds(offset, 128)],
                            (8, 128),
                        )
                        for q in range(2)
                    ]
                    return jnp.concatenate(parts, axis=0).astype(BF16)

                near, far = source(0), source(128)
                low = jnp.where(in_low, take(near, at_low), take(far, at_low)).astype(F32)
                high = jnp.where(in_high, take(near, at_high), take(far, at_high)).astype(F32)
                for q in range(2):
                    z = 2 * pair + q
                    half = slice(8 * q, 8 * q + 8)
                    total[z] = total[z] + (w_low * low[half] + w_high * high[half])
        for z in range(DEPTH):
            out[z, :, here] = total[z]


def step_kernel(
    sino,
    angles,
    w_first,
    b_first,
    w_second,
    b_second,
    pred_out,
    target_out,
    grads_out,
    views,
    send,
    recv,
    windows,
    own,
    first_cat,
    second_cat,
    second_t,
    gather_first,
    gather_second,
    field,
    eighths,
    piece,
    totals,
    near_u,
    patch_u,
    hidden_all,
    taps,
    near_r,
    acc_first,
    acc_second,
    part_slots,
    whole_slots,
    mine,
    local_sem,
    data_send,
    data_recv,
    halo_send,
    halo_recv,
    part_send,
    part_recv,
    tot_send,
    tot_recv,
    slab_send,
    slab_recv,
    pair_send,
    pair_recv,
):
    sub, half, slab = lax.axis_index("sub"), lax.axis_index("half"), lax.axis_index("slab")
    me = half * SLABS + slab
    pair = sub * 2 + half

    def ring(other):
        return (sub, other // SLABS, lax.rem(other, SLABS))

    def slab_peer(p):
        other = lax.rem(slab + p, SLABS)
        return other, (sub, half, other)

    def pair_peer(p):
        other = lax.rem(pair + p, 2 * SUBS)
        return other, (other // 2, lax.rem(other, 2), slab)

    def sub_peer(p):
        other = lax.rem(sub + p, SUBS)
        return other, (other, half, slab)

    def group_peer(p):
        other = lax.rem(me + p, GROUP)
        return other, ring(other)

    def greet(peer):
        def step(p, carry):
            pl.semaphore_signal(
                pltpu.get_barrier_semaphore(), inc=1, device_id=peer(p)[1], device_id_type=MESH
            )
            return carry

        return step

    load = pltpu.make_async_copy(
        sino.at[:, :, pl.ds(FIRST_COL, COLS)], views, local_sem.at[0]
    )
    load.start()
    lax.fori_loop(1, GROUP, greet(group_peer), 0)
    lax.fori_loop(1, 2 * SUBS, greet(pair_peer), 0)
    load.wait()

    pieces = view_pieces(angles)
    spare = iota((8, 128), 1) < 4

    def pack(q, carry):
        at = pl.multiple_of(q * 16, 16)
        zero = views[0, pl.ds(at, 16), :].astype(F32)
        one = views[1, pl.ds(at, 16), :].astype(F32)
        for i in range(4):
            both = jnp.concatenate([zero[4 * i : 4 * i + 4], one[4 * i : 4 * i + 4]], axis=0)
            start = jnp.where(spare, pieces, both[:, :128])
            both = jnp.concatenate([start, both[:, 128:]], axis=1)
            send[4 * q + i] = jnp.concatenate(
                [both[:, : COLS // 2], both[:, COLS // 2 :]], axis=0
            ).astype(BF16)
        return carry

    lax.fori_loop(0, GROUP // 4, pack, 0)
    recv[me] = send[me]
    own[...] = jnp.zeros_like(own)
    first_cat[...] = build_first(w_first[...], b_first[...])
    second_cat[...], second_t[...] = build_second(w_second[...])
    gather_first[...], gather_second[...] = build_gather()
    pl.semaphore_wait(pltpu.get_barrier_semaphore(), GROUP - 1 + 2 * SUBS - 1)

    def remote(src, dst, send_sem, recv_sem, target):
        return pltpu.make_async_remote_copy(
            src_ref=src,
            dst_ref=dst,
            send_sem=send_sem,
            recv_sem=recv_sem,
            device_id=target,
            device_id_type=MESH,
        )

    def data_copy(other, slot):
        return remote(
            send.at[other], recv.at[slot], data_send.at[other], data_recv.at[slot], ring(other)
        )

    def start(p, carry):
        other = lax.rem(me + p, GROUP)
        data_copy(other, me).start()
        return carry

    lax.fori_loop(1, GROUP, start, 0)

    def one_sender(p, carry):
        other = lax.rem(me + GROUP - p, GROUP)

        @pl.when(p > 0)
        def _():
            data_copy(other, other).wait_recv()

        add_sender(recv[other], windows, own)
        return carry

    lax.fori_loop(0, GROUP, one_sender, 0)
    own[...] = own[...] * (math.pi / VPS)

    to_after = remote(
        own.at[2:4], field.at[0:2], halo_send.at[0], halo_recv.at[0], group_peer(1)[1]
    )
    to_before = remote(
        own.at[0:2], field.at[6:8], halo_send.at[1], halo_recv.at[1], group_peer(GROUP - 1)[1]
    )
    to_after.start()
    to_before.start()

    def eighth(index):
        return pl.ds(pl.multiple_of(index * 128, 128), 128)

    def part_copy(p, arriving):
        other, target = sub_peer(p)
        slot = other if arriving else sub
        return remote(
            own.at[:, :, eighth(other)],
            eighths.at[slot],
            part_send.at[other],
            part_recv.at[slot],
            target,
        )

    def total_copy(p, arriving):
        other, target = sub_peer(p)
        slot = other if arriving else sub
        return remote(
            piece, totals.at[:, :, eighth(slot)], tot_send.at[other], tot_recv.at[slot], target
        )

    def slab_copy(p, arriving):
        other, target = slab_peer(p)
        slot = other if arriving else slab
        return remote(
            mine.at[0], part_slots.at[slot], slab_send.at[other], slab_recv.at[slot], target
        )

    def pair_copy(p, arriving):
        other, target = pair_peer(p)
        slot = other if arriving else pair
        return remote(
            mine.at[1], whole_slots.at[slot], pair_send.at[other], pair_recv.at[slot], target
        )

    def started(make, count):
        def step(p, carry):
            make(p, False).start()
            return carry

        lax.fori_loop(1, count, step, 0)

    def finished(make, count):
        def step(p, carry):
            make(p, True).wait()
            return carry

        lax.fori_loop(1, count, step, 0)

    started(part_copy, SUBS)
    eighths[sub] = own[:, :, eighth(sub)]
    taps[...] = jnp.zeros_like(taps)
    near_r[...] = jnp.zeros_like(near_r)
    acc_first[...] = jnp.zeros_like(acc_first)
    acc_second[...] = jnp.zeros_like(acc_second)
    ones = (iota((8, X), 0) == 0).astype(F32)

    def place(m, value):
        near_u[m] = jnp.concatenate([shifted(value, 1), value, shifted(value, -1)], axis=0)

    def forward(j, carry):
        patch = jnp.concatenate([near_u[j], near_u[j + 1], near_u[j + 2], ones], axis=0)
        high, low = split(patch)
        patch_u[j] = high
        pre = jnp.dot(
            first_cat[...], jnp.concatenate([high, high, low], axis=0), preferred_element_type=F32
        )
        outside = ((j == 0) & (me == 0)) | ((j == 5) & (me == GROUP - 1))
        hidden = jnp.maximum(pre, 0.0) * jnp.where(outside, 0.0, 1.0)
        high, low = split(hidden)
        hidden_all[j] = high
        main = jnp.dot(second_t[...], high, preferred_element_type=F32)
        rest = jnp.dot(second_t[0:PATCH], low, preferred_element_type=F32)
        added = main[:72] + (main[PATCH : PATCH + 72] + rest[:72])
        for shift_z in range(3):
            at = j - shift_z + 2
            taps[at] = taps[at] + added[24 * shift_z : 24 * shift_z + 24]
        return carry

    for i in range(DEPTH):
        place(i + 2, own[i])
    lax.fori_loop(2, 4, forward, 0)
    finished(part_copy, SUBS)
    total = eighths[0]
    for s in range(1, SUBS):
        total = total + eighths[s]
    piece[...] = total
    totals[:, :, eighth(sub)] = total
    started(total_copy, SUBS)
    to_after.wait()
    to_before.wait()
    for m in range(2):
        place(m, jnp.where(me > 0, field[m], 0.0))
        place(m + 6, jnp.where(me < GROUP - 1, field[m + 6], 0.0))
    lax.fori_loop(0, 2, forward, 0)
    lax.fori_loop(4, 6, forward, 0)
    finished(total_copy, SUBS)

    sum_square = jnp.zeros((8, X), F32)
    sum_resid = jnp.zeros((8, X), F32)
    for i in range(DEPTH):
        value = own[i]
        conv = shifted(taps[i + 2, 0:8], 1) + taps[i + 2, 8:16] + shifted(taps[i + 2, 16:24], -1)
        pred = value + conv + b_second[0]
        target = (totals[i] - value) / (SUBS - 1)
        pred_out[i] = pred
        target_out[i] = target
        diff = pred - target
        resid = (2.0 * diff) / CELLS
        sum_square = sum_square + diff * diff
        sum_resid = sum_resid + resid
        near_r[i + 2] = jnp.concatenate([shifted(resid, -1), resid, shifted(resid, 1)], axis=0)

    nothing = jnp.zeros((8, X), F32)

    def backward(j, carry):
        patch = jnp.concatenate([near_r[j + 2], near_r[j + 1], near_r[j], nothing], axis=0)
        high, low = split(patch)
        grad = jnp.dot(
            second_cat[...], jnp.concatenate([high, high, low], axis=0), preferred_element_type=F32
        )
        hidden = hidden_all[j]
        acc_second[:, :PATCH] += dot_nt(hidden, high)
        grad = jnp.where(hidden.astype(F32) > 0.0, grad, 0.0).astype(BF16)
        acc_first[:, :PATCH] += dot_nt(grad, patch_u[j])
        return carry

    lax.fori_loop(0, 6, backward, 0)

    packed = gathered(acc_first[...], gather_first[...])
    packed = packed + gathered(acc_second[...], gather_second[...])
    packed = packed[:16] + pltpu.roll(packed[16:], 64, 1)
    row, lane = iota((16, 128), 0), iota((16, 128), 1)
    packed = packed + jnp.where((row == 0) & (lane == 60), jnp.sum(sum_square) / CELLS, 0.0)
    packed = packed + jnp.where((row == 0) & (lane == 61), jnp.sum(sum_resid), 0.0)

    mine[0] = packed
    part_slots[slab] = packed
    started(slab_copy, SLABS)
    finished(slab_copy, SLABS)
    packed = part_slots[0]
    for s in range(1, 16):
        packed = packed + part_slots[s]
    mine[1] = packed
    whole_slots[pair] = packed
    started(pair_copy, 2 * SUBS)
    finished(pair_copy, 2 * SUBS)
    packed = whole_slots[0]
    for s in range(1, 16):
        packed = packed + whole_slots[s]
    grads_out[...] = packed

    def sent(p, carry):
        other = lax.rem(me + p, GROUP)
        data_copy(other, me).wait_send()
        return carry

    lax.fori_loop(1, GROUP, sent, 0)


def finish_kernel(pred, target, packed, pred_out, target_out, loss, g_w1, g_b1, g_w2, g_b2, sems):
    copies = [
        pltpu.make_async_copy(pred, pred_out, sems.at[0]),
        pltpu.make_async_copy(target, target_out, sems.at[1]),
    ]
    for copy in copies:
        copy.start()
    value = packed[...]
    both = jnp.concatenate([value, pltpu.roll(value, 64, 1)], axis=0)
    g_w1[...] = both[:, :27]
    g_w2[...] = both[:, 32:59]
    row, lane = iota((CH, 128), 0), iota((CH, 128), 1)
    column = jnp.sum(jnp.where(lane == 27, both, 0.0), axis=1, keepdims=True)
    g_b1[...] = jnp.sum(jnp.where(lane == row, column, 0.0), axis=0, keepdims=True)[:, :CH]
    loss[...] = value[0:1, 60:61]
    g_b2[...] = value[0:1, 61:62]
    for copy in copies:
        copy.wait()


VMEM = pl.BlockSpec(memory_space=pltpu.VMEM)
SMEM = pl.BlockSpec(memory_space=pltpu.SMEM)
ANY = pl.BlockSpec(memory_space=pl.ANY)
HBM = pl.BlockSpec(memory_space=pltpu.HBM)


def shape(dims, dtype=F32):
    return jax.ShapeDtypeStruct(dims, dtype)


def body(sinogram, angles, w_first, b_first, w_second, b_second):
    dma = pltpu.SemaphoreType.DMA
    vmem = pltpu.VMEM
    pred, target, grads = pl.pallas_call(
        step_kernel,
        name="train_step",
        out_shape=(shape((DEPTH, Y, X)), shape((DEPTH, Y, X)), shape((16, 128))),
        in_specs=[HBM, SMEM] + [VMEM] * 3 + [SMEM],
        out_specs=[VMEM] * 3,
        scratch_shapes=[
            vmem((2, 128, COLS), BF16),
            vmem((GROUP, 16, COLS // 2), BF16),
            vmem((GROUP, 16, COLS // 2), BF16),
            vmem((X // 128, 8, 256), F32),
            vmem((DEPTH, Y, X), F32),
            vmem((256, 3 * PATCH), BF16),
            vmem((256, 3 * PATCH), BF16),
            vmem((2 * PATCH, 256), BF16),
            vmem((1024, 128), BF16),
            vmem((1024, 128), BF16),
            vmem((8, Y, X), F32),
            vmem((SUBS, DEPTH, Y, 128), F32),
            vmem((DEPTH, Y, 128), F32),
            vmem((DEPTH, Y, X), F32),
            vmem((8, 24, X), F32),
            vmem((6, PATCH, X), BF16),
            vmem((6, 256, X), BF16),
            vmem((8, 24, X), F32),
            vmem((8, 24, X), F32),
            vmem((256, 128), F32),
            vmem((256, 128), F32),
            vmem((16, 16, 128), F32),
            vmem((16, 16, 128), F32),
            vmem((2, 16, 128), F32),
            dma((1,)),
            dma((GROUP,)),
            dma((GROUP,)),
            dma((2,)),
            dma((2,)),
        ]
        + [dma((SUBS,))] * 4
        + [dma((16,))] * 4,
        compiler_params=pltpu.CompilerParams(
            collective_id=0, has_side_effects=True, vmem_limit_bytes=62 << 20
        ),
    )(sinogram, angles, w_first, b_first[None], w_second, b_second)
    pred, target, loss, g_w1, g_b1, g_w2, g_b2 = pl.pallas_call(
        finish_kernel,
        name="finish",
        out_shape=(
            shape((1, DEPTH, Y, X)),
            shape((1, DEPTH, Y, X)),
            shape((1, 1)),
            shape((CH, 27)),
            shape((1, CH)),
            shape((CH, 27)),
            shape((1, 1)),
        ),
        in_specs=[VMEM] * 3,
        out_specs=[ANY] * 2 + [VMEM] * 5,
        scratch_shapes=[dma((2,))],
        compiler_params=pltpu.CompilerParams(vmem_limit_bytes=62 << 20),
    )(pred[None], target[None], grads)
    return pred, target, loss.reshape(()), g_w1, g_b1.reshape(CH), g_w2, g_b2.reshape(1)


def solution(mesh):
    finer = Mesh(mesh.devices.reshape(SUBS, 2, SLABS), ("sub", "half", "slab"))
    every = ("sub", "half", "slab")
    return jax.shard_map(
        body,
        mesh=finer,
        in_specs=(P(every, None, None), P(every), P(), P(), P(), P()),
        out_specs=(
            P(("sub", "half"), "slab", None, None),
            P(("sub", "half"), "slab", None, None),
            P(),
            P(),
            P(),
            P(),
            P(),
        ),
        check_vma=False,
    )
```

time: 96.3 us -> 66.5 us (0.69)
  Pallas kernels: 88.8 us -> 65 us
  local copies, waits for them, and re-layouts: 5.76 us -> 0 us
    pallas_call x3 -> x2, Pallas kernels: 88.8 us -> 65 us  [the longest x1 62.7 us: body(): pl.pallas_call(step_kernel, name='train_step', out_shape=(shape((DEPTH, Y...]
    unnamed x10 -> x0, local copies, waits for them, and re-layouts: 2.8 us -> none
    slice x3 -> x0, local copies, waits for them, and re-layouts: 1.96 us -> none  [the longest x1 0.69 us: body(): grads[:, 27]]
where the time goes in v2:
time: 66.5 us; the launch traced here: 66.2 us
  Pallas kernels  65 us (98%)
  between operations  1.29 us (2%)
    pallas_call x1, Pallas kernels, body(): pl.pallas_call(step_kernel, name='train_step', out_shape=(shape((DEPTH, Y...  62.7 us
    pallas_call x1, Pallas kernels, body(): pl.pallas_call(finish_kernel, name='finish', out_shape=(shape((1, DEPTH,...  2.3 us

profile of v2, /device:TPU:1, one launch (start us, length us, event | category | flops | bytes accessed | tf_op | source)
XLA Modules:
  0.0 66.2 jit_solution(18267132758734759537)
XLA Ops:
  1.3 62.7 %train_step.1 = (f32[4,8,1024]{2,1,0:T(8,128)}, f32[4,8,1024]{2,1,0:T(8,128)}, f32[16,128]{1,0:T(8,128)}) custom-call(bf16[2,128,2048]{2,1,0:T(8,128)(2,1)} %sino.1, f32[2]{0:T(128)} %angles.1, f32[32,27]{1,0:T(8,128)} %w_first.1, f32[1,32]{1,0:T(1,128)} %bitcast.8, f32[32,27]{1,0:T(8,128)} %w_second.1, f32[1]{0:T(128)S(6)} %copy.13.b_second), custom_call_target="tpu_custom_call" | custom-call | tf_op jit(solution)/shard_map/train_step/pallas_call | solution.py:578
  63.9 2.3 %finish.1 = (f32[1,4,8,1024]{3,2,1,0:T(8,128)}, f32[1,4,8,1024]{3,2,1,0:T(8,128)}, f32[1,1]{1,0:T(1,128)}, f32[32,27]{1,0:T(8,128)}, f32[1,32]{1,0:T(1,128)}, /*index=5*/f32[32,27]{1,0:T(8,128)}, f32[1,1]{1,0:T(1,128)}) custom-call(f32[1,4,8,1024]{3,2,1,0:T(8,128)} %bitcast.6, f32[1,4,8,1024]{3,2,1,0:T(8,128)} %bitcast.7, f32[16,128]{1,0:T(8,128)} %get-tuple-element.19.packed), custom_call_target="tpu_custom_call" | custom-call | tf_op jit(solution)/shard_map/finish/pallas_call | solution.py:621

commit v3 on v2

--- a/solution.py
+++ b/solution.py
@@ -279,39 +279,63 @@
     pair = sub * 2 + half
 
     def ring(other):
-        return (sub, other // SLABS, lax.rem(other, SLABS))
+        return (sub, other >> 4, other & 15)
+
+    far_first = (2, 1, 3, 0)
 
     def slab_peer(p):
-        other = lax.rem(slab + p, SLABS)
+        y = ((slab >> 2) + far_first[p >> 2]) & 3
+        other = y * 4 + ((slab + far_first[p & 3]) & 3)
         return other, (sub, half, other)
 
+    def sub_at(p):
+        x = ((sub >> 1) + far_first[p >> 1]) & 3
+        return x * 2 + ((sub + 1 + p) & 1)
+
     def pair_peer(p):
-        other = lax.rem(pair + p, 2 * SUBS)
-        return other, (other // 2, lax.rem(other, 2), slab)
+        other_sub, other_half = sub_at(p >> 1), (half + 1 + p) & 1
+        return other_sub * 2 + other_half, (other_sub, other_half, slab)
 
     def sub_peer(p):
-        other = lax.rem(sub + p, SUBS)
+        other = sub_at(p)
         return other, (other, half, slab)
 
+    def distance(p):
+        if p < 8:
+            return p & 1, p >> 1, 0
+        q = p - 8
+        return (q // 3) & 1, q // 6, far_first[q % 3]
+
+    def group_target(p):
+        core, y, z = distance(p)
+        return ((half + core) & 1) * SLABS + (((slab >> 2) + y) & 3) * 4 + ((slab + z) & 3)
+
+    def group_source(p):
+        q = p - 8
+        third = lax.rem(q, 3)
+        near = p < 8
+        core = jnp.where(near, p, q // 3) & 1
+        y = jnp.where(near, p >> 1, q // 6)
+        z = jnp.where(near, 0, jnp.where(third == 0, 2, jnp.where(third == 1, 1, 3)))
+        row = ((slab >> 2) + 4 - y) & 3
+        return ((half + core) & 1) * SLABS + row * 4 + ((slab + 4 - z) & 3)
+
     def group_peer(p):
-        other = lax.rem(me + p, GROUP)
+        other = group_target(GROUP - 1 - p)
         return other, ring(other)
 
-    def greet(peer):
-        def step(p, carry):
+    def greet(peer, count):
+        for p in range(count - 1):
             pl.semaphore_signal(
                 pltpu.get_barrier_semaphore(), inc=1, device_id=peer(p)[1], device_id_type=MESH
             )
-            return carry
-
-        return step
 
     load = pltpu.make_async_copy(
         sino.at[:, :, pl.ds(FIRST_COL, COLS)], views, local_sem.at[0]
     )
     load.start()
-    lax.fori_loop(1, GROUP, greet(group_peer), 0)
-    lax.fori_loop(1, 2 * SUBS, greet(pair_peer), 0)
+    greet(group_peer, GROUP)
+    greet(pair_peer, 2 * SUBS)
     load.wait()
 
     pieces = view_pieces(angles)
@@ -353,15 +377,11 @@
             send.at[other], recv.at[slot], data_send.at[other], data_recv.at[slot], ring(other)
         )
 
-    def start(p, carry):
-        other = lax.rem(me + p, GROUP)
-        data_copy(other, me).start()
-        return carry
-
-    lax.fori_loop(1, GROUP, start, 0)
+    for p in range(1, GROUP):
+        data_copy(group_target(p), me).start()
 
     def one_sender(p, carry):
-        other = lax.rem(me + GROUP - p, GROUP)
+        other = group_source(p)
 
         @pl.when(p > 0)
         def _():
@@ -374,13 +394,11 @@
     own[...] = own[...] * (math.pi / VPS)
 
     to_after = remote(
-        own.at[2:4], field.at[0:2], halo_send.at[0], halo_recv.at[0], group_peer(1)[1]
+        own.at[2:4], field.at[0:2], halo_send.at[0], halo_recv.at[0], ring(lax.rem(me + 1, GROUP))
     )
     to_before = remote(
-        own.at[0:2], field.at[6:8], halo_send.at[1], halo_recv.at[1], group_peer(GROUP - 1)[1]
+        own.at[0:2], field.at[6:8], halo_send.at[1], halo_recv.at[1], ring(lax.rem(me + GROUP - 1, GROUP))
     )
-    to_after.start()
-    to_before.start()
 
     def eighth(index):
         return pl.ds(pl.multiple_of(index * 128, 128), 128)
@@ -418,20 +436,16 @@
         )
 
     def started(make, count):
-        def step(p, carry):
+        for p in range(count - 1):
             make(p, False).start()
-            return carry
-
-        lax.fori_loop(1, count, step, 0)
 
     def finished(make, count):
-        def step(p, carry):
+        for p in range(count - 1):
             make(p, True).wait()
-            return carry
-
-        lax.fori_loop(1, count, step, 0)
 
     started(part_copy, SUBS)
+    to_after.start()
+    to_before.start()
     eighths[sub] = own[:, :, eighth(sub)]
     taps[...] = jnp.zeros_like(taps)
     near_r[...] = jnp.zeros_like(near_r)
@@ -509,7 +523,7 @@
         acc_first[:, :PATCH] += dot_nt(grad, patch_u[j])
         return carry
 
-    lax.fori_loop(0, 6, backward, 0)
+    lax.fori_loop(0, 6, backward, 0, unroll=2)
 
     packed = gathered(acc_first[...], gather_first[...])
     packed = packed + gathered(acc_second[...], gather_second[...])

time: 66.5 us -> 63.2 us (0.950)
  Pallas kernels: 65 us -> 61.7 us
    pallas_call x1, Pallas kernels: 62.7 us -> 59.4 us  [body(): pl.pallas_call(step_kernel, name='train_step', out_shape=(shape((DEPTH, Y...]
where the time goes in v3:
time: 63.2 us; the launch traced here: 63 us
  Pallas kernels  61.7 us (98%)
  between operations  1.29 us (2%)
    pallas_call x1, Pallas kernels, body(): pl.pallas_call(step_kernel, name='train_step', out_shape=(shape((DEPTH, Y...  59.4 us
    pallas_call x1, Pallas kernels, body(): pl.pallas_call(finish_kernel, name='finish', out_shape=(shape((1, DEPTH,...  2.3 us

profile of v3, /device:TPU:1, one launch (start us, length us, event | category | flops | bytes accessed | tf_op | source)
XLA Modules:
  0.0 63.0 jit_solution(18028508389160951581)
XLA Ops:
  1.3 59.4 %train_step.1 = (f32[4,8,1024]{2,1,0:T(8,128)}, f32[4,8,1024]{2,1,0:T(8,128)}, f32[16,128]{1,0:T(8,128)}) custom-call(bf16[2,128,2048]{2,1,0:T(8,128)(2,1)} %sino.1, f32[2]{0:T(128)} %angles.1, f32[32,27]{1,0:T(8,128)} %w_first.1, f32[1,32]{1,0:T(1,128)} %bitcast.8, f32[32,27]{1,0:T(8,128)} %w_second.1, f32[1]{0:T(128)S(6)} %copy.13.b_second), custom_call_target="tpu_custom_call" | custom-call | tf_op jit(solution)/shard_map/train_step/pallas_call | solution.py:592
  60.7 2.3 %finish.1 = (f32[1,4,8,1024]{3,2,1,0:T(8,128)}, f32[1,4,8,1024]{3,2,1,0:T(8,128)}, f32[1,1]{1,0:T(1,128)}, f32[32,27]{1,0:T(8,128)}, f32[1,32]{1,0:T(1,128)}, /*index=5*/f32[32,27]{1,0:T(8,128)}, f32[1,1]{1,0:T(1,128)}) custom-call(f32[1,4,8,1024]{3,2,1,0:T(8,128)} %bitcast.6, f32[1,4,8,1024]{3,2,1,0:T(8,128)} %bitcast.7, f32[16,128]{1,0:T(8,128)} %get-tuple-element.19.packed), custom_call_target="tpu_custom_call" | custom-call | tf_op jit(solution)/shard_map/finish/pallas_call | solution.py:635

commit v4 on v3

--- a/solution.py
+++ b/solution.py
@@ -132,31 +132,32 @@
     )
 
 
-def view_pieces(angles):
+def view_table(angles):
     lane, row = iota((8, 128), 1), iota((8, 128), 0)
     angle = jnp.where(lane < 2, angles[0], angles[1])
     value = jnp.where(lane & 1 == 0, jnp.cos(angle), jnp.sin(angle))
-    high = value.astype(BF16).astype(F32)
-    middle = (value - high).astype(BF16).astype(F32)
-    low = value - high - middle
-    out = jnp.where(row == 0, high, jnp.where(row == 1, middle, jnp.where(row == 2, low, 0.0)))
-    return jnp.where(lane < 4, out, 0.0)
+    return jnp.where((row == 0) & (lane < 4), value, 0.0)
+
+
+def every_lane(source, index):
+    return take(source, jnp.full((8, 128), index, jnp.int32))
 
 
 def window_range(part_x):
     ends = (abs(128 * part_x - 511.5), abs(128 * part_x - 384.5))
     middle = (DET - 1) / 2.0
-    first = (math.floor(middle - max(ends) - 4.0) - FIRST_COL - 1) // 64
-    last = (math.floor(middle + min(ends) + 0.5) - FIRST_COL - 1) // 64
+    first = (math.floor(middle - max(ends) - 4.0) - FIRST_COL) // 64
+    last = (math.floor(middle + min(ends) + 0.5) - FIRST_COL) // 64
     return first, last
 
 
-def add_sender(block, windows, out):
+def add_sender(block, extra, windows, out):
     value = block.astype(F32)
-    row = jnp.concatenate([value[:8], value[8:]], axis=1)
+    tables = jnp.broadcast_to(extra, (8, 128))
+    ends = [take(tables, iota((8, 128), 0) + at) for at in (8, 16)]
+    row = jnp.concatenate([ends[0], value[:8], value[8:], ends[1]], axis=1)
     moved = pltpu.roll(row, COLS - 64, 1)
-    tables = jnp.broadcast_to(value[0:1, :128] + value[1:2, :128] + value[2:3, :128], (8, 128))
-    views = [take(tables, jnp.full((8, 128), i, jnp.int32)) for i in range(4)]
+    views = [every_lane(tables, i) for i in range(4)]
     row_index = iota((8, 128), 0)
     row_pos = row_index.astype(F32) - (Y - 1) / 2.0
     lane = iota((8, 128), 1).astype(F32)
@@ -165,25 +166,32 @@
         source = moved if k & 1 else row
         return source[:, (k >> 1) * 128 : (k >> 1) * 128 + 128]
 
-    steps = []
+    lowest = []
     for part_x in range(X // 128):
         begin = 128.0 * part_x - (X - 1) / 2.0
         both = []
         for v in range(2):
             cosine, sine = views[2 * v], views[2 * v + 1]
             least = jnp.minimum(begin * cosine, (begin + 127.0) * cosine)
-            least = (least - 3.5 * jnp.abs(sine)) + (DET - 1) / 2.0
-            both.append(jnp.floor((jnp.floor(least) - (FIRST_COL + 1.0)) * (1.0 / 64.0)))
-        steps.append(both)
-        step = jnp.where(row_index < 4, both[0], both[1])
+            both.append(jnp.floor((least - 3.5 * jnp.abs(sine)) + (DET - 1) / 2.0))
+        lowest.append(both)
+        offset = jnp.where(row_index < 4, both[0], both[1]) - float(FIRST_COL)
+        step = jnp.floor(offset * (1.0 / 64.0))
         first, last = window_range(part_x)
         near, far = piece(first), piece(first + 2)
         for k in range(first + 1, last + 1):
             reached = step >= float(k)
             near = jnp.where(reached, piece(k), near)
             far = jnp.where(reached, piece(k + 2), far)
-        windows[part_x, :, :128] = near
-        windows[part_x, :, 128:] = far
+        moved_by = (offset - 64.0 * step).astype(jnp.int32)
+        place = moved_by + iota((8, 128), 1)
+        at = place & 127
+        window = [
+            jnp.where(place < 128, take(near, at), take(far, at)),
+            take(far, moved_by),
+            take(far, moved_by + 1),
+        ]
+        windows[part_x] = jnp.concatenate(window, axis=1)
     for part_x in range(X // 128):
         here = slice(part_x * 128, (part_x + 1) * 128)
         total = [out[z, :, here] for z in range(DEPTH)]
@@ -196,7 +204,7 @@
             part = pos - lower
             w_high = part.astype(BF16).astype(F32)
             w_low = (1.0 - part).astype(BF16).astype(F32)
-            index = (lower - (64.0 * steps[part_x][v] + FIRST_COL)).astype(jnp.int32)
+            index = (lower - lowest[part_x][v]).astype(jnp.int32)
             index = jnp.concatenate([index, index], axis=0)
             at_low = (index & 127).astype(jnp.int16)
             at_high = ((index + 1) & 127).astype(jnp.int16)
@@ -206,18 +214,19 @@
             for pair in range(2):
 
                 def source(offset):
+                    first_row = v * 4 + 2 * pair
                     parts = [
                         jnp.broadcast_to(
-                            windows[part_x, pl.ds(v * 4 + 2 * pair + q, 1), pl.ds(offset, 128)],
-                            (8, 128),
+                            windows[part_x, pl.ds(first_row + q, 1), pl.ds(offset, 128)], (8, 128)
                         )
                         for q in range(2)
                     ]
                     return jnp.concatenate(parts, axis=0).astype(BF16)
 
-                near, far = source(0), source(128)
-                low = jnp.where(in_low, take(near, at_low), take(far, at_low)).astype(F32)
-                high = jnp.where(in_high, take(near, at_high), take(far, at_high)).astype(F32)
+                near, next_one, after = source(0), source(128), source(256)
+                low = jnp.where(in_low, take(near, at_low), next_one).astype(F32)
+                high = jnp.where(in_low, next_one, after)
+                high = jnp.where(in_high, take(near, at_high), high).astype(F32)
                 for q in range(2):
                     z = 2 * pair + q
                     half = slice(8 * q, 8 * q + 8)
@@ -239,6 +248,8 @@
     views,
     send,
     recv,
+    send_extra,
+    recv_extra,
     windows,
     own,
     first_cat,
@@ -263,6 +274,8 @@
     local_sem,
     data_send,
     data_recv,
+    extra_send,
+    extra_recv,
     halo_send,
     halo_recv,
     part_send,
@@ -338,8 +351,8 @@
     greet(pair_peer, 2 * SUBS)
     load.wait()
 
-    pieces = view_pieces(angles)
-    spare = iota((8, 128), 1) < 4
+    table = view_table(angles)
+    lane, row = iota((8, 128), 1), iota((8, 128), 0)
 
     def pack(q, carry):
         at = pl.multiple_of(q * 16, 16)
@@ -347,15 +360,18 @@
         one = views[1, pl.ds(at, 16), :].astype(F32)
         for i in range(4):
             both = jnp.concatenate([zero[4 * i : 4 * i + 4], one[4 * i : 4 * i + 4]], axis=0)
-            start = jnp.where(spare, pieces, both[:, :128])
-            both = jnp.concatenate([start, both[:, 128:]], axis=1)
-            send[4 * q + i] = jnp.concatenate(
-                [both[:, : COLS // 2], both[:, COLS // 2 :]], axis=0
-            ).astype(BF16)
+            ends = every_lane(both[:, :128], 127), every_lane(both[:, 1152:], 0)
+            line = jnp.where(lane == row + 8, ends[0], table)
+            line = jnp.where(lane == row + 16, ends[1], line)
+            send_extra[4 * q + i] = jnp.sum(line, axis=0, keepdims=True)
+            send[4 * q + i] = jnp.concatenate([both[:, 128:640], both[:, 640:1152]], axis=0).astype(
+                BF16
+            )
         return carry
 
     lax.fori_loop(0, GROUP // 4, pack, 0)
     recv[me] = send[me]
+    recv_extra[me] = send_extra[me]
     own[...] = jnp.zeros_like(own)
     first_cat[...] = build_first(w_first[...], b_first[...])
     second_cat[...], second_t[...] = build_second(w_second[...])
@@ -377,20 +393,37 @@
             send.at[other], recv.at[slot], data_send.at[other], data_recv.at[slot], ring(other)
         )
 
+    def extra_copy(other, slot):
+        return remote(
+            send_extra.at[other],
+            recv_extra.at[slot],
+            extra_send.at[other],
+            extra_recv.at[slot],
+            ring(other),
+        )
+
     for p in range(1, GROUP):
+        extra_copy(group_target(p), me).start()
         data_copy(group_target(p), me).start()
 
-    def one_sender(p, carry):
-        other = group_source(p)
-
-        @pl.when(p > 0)
-        def _():
-            data_copy(other, other).wait_recv()
-
-        add_sender(recv[other], windows, own)
+    def two_senders(p, carry):
+        for q in range(2):
+            other = group_source(2 * p + q)
+
+            def arrived(other=other):
+                extra_copy(other, other).wait_recv()
+                data_copy(other, other).wait_recv()
+
+            if q == 0:
+                pl.when(p > 0)(arrived)
+            else:
+                arrived()
+        for q in range(2):
+            other = group_source(2 * p + q)
+            add_sender(recv[other], recv_extra[other], windows.at[q], own)
         return carry
 
-    lax.fori_loop(0, GROUP, one_sender, 0)
+    lax.fori_loop(0, GROUP // 2, two_senders, 0)
     own[...] = own[...] * (math.pi / VPS)
 
     to_after = remote(
@@ -550,6 +583,7 @@
 
     def sent(p, carry):
         other = lax.rem(me + p, GROUP)
+        extra_copy(other, me).wait_send()
         data_copy(other, me).wait_send()
         return carry
 
@@ -597,9 +631,11 @@
         out_specs=[VMEM] * 3,
         scratch_shapes=[
             vmem((2, 128, COLS), BF16),
-            vmem((GROUP, 16, COLS // 2), BF16),
-            vmem((GROUP, 16, COLS // 2), BF16),
-            vmem((X // 128, 8, 256), F32),
+            vmem((GROUP, 16, X // 2), BF16),
+            vmem((GROUP, 16, X // 2), BF16),
+            vmem((GROUP, 1, 128), F32),
+            vmem((GROUP, 1, 128), F32),
+            vmem((2, X // 128, 8, 384), F32),
             vmem((DEPTH, Y, X), F32),
             vmem((256, 3 * PATCH), BF16),
             vmem((256, 3 * PATCH), BF16),
@@ -621,6 +657,8 @@
             vmem((16, 16, 128), F32),
             vmem((2, 16, 128), F32),
             dma((1,)),
+            dma((GROUP,)),
+            dma((GROUP,)),
             dma((GROUP,)),
             dma((GROUP,)),
             dma((2,)),

time: 63.2 us -> 61.2 us (0.968)
  Pallas kernels: 61.7 us -> 59.7 us
    pallas_call x1, Pallas kernels: 59.4 us -> 57.4 us  [body(): pl.pallas_call(step_kernel, name='train_step', out_shape=(shape((DEPTH, Y...]
where the time goes in v4:
time: 61.2 us; the launch traced here: 61 us
  Pallas kernels  59.7 us (98%)
  between operations  1.29 us (2%)
    pallas_call x1, Pallas kernels, body(): pl.pallas_call(step_kernel, name='train_step', out_shape=(shape((DEPTH, Y...  57.4 us
    pallas_call x1, Pallas kernels, body(): pl.pallas_call(finish_kernel, name='finish', out_shape=(shape((1, DEPTH,...  2.3 us

profile of v4, /device:TPU:1, one launch (start us, length us, event | category | flops | bytes accessed | tf_op | source)
XLA Modules:
  0.0 61.0 jit_solution(9166008967718913323)
XLA Ops:
  1.3 57.4 %train_step.1 = (f32[4,8,1024]{2,1,0:T(8,128)}, f32[4,8,1024]{2,1,0:T(8,128)}, f32[16,128]{1,0:T(8,128)}) custom-call(bf16[2,128,2048]{2,1,0:T(8,128)(2,1)} %sino.1, f32[2]{0:T(128)} %angles.1, f32[32,27]{1,0:T(8,128)} %w_first.1, f32[1,32]{1,0:T(1,128)} %bitcast.8, f32[32,27]{1,0:T(8,128)} %w_second.1, f32[1]{0:T(128)S(6)} %copy.13.b_second), custom_call_target="tpu_custom_call" | custom-call | tf_op jit(solution)/shard_map/train_step/pallas_call | solution.py:626
  58.7 2.3 %finish.1 = (f32[1,4,8,1024]{3,2,1,0:T(8,128)}, f32[1,4,8,1024]{3,2,1,0:T(8,128)}, f32[1,1]{1,0:T(1,128)}, f32[32,27]{1,0:T(8,128)}, f32[1,32]{1,0:T(1,128)}, /*index=5*/f32[32,27]{1,0:T(8,128)}, f32[1,1]{1,0:T(1,128)}) custom-call(f32[1,4,8,1024]{3,2,1,0:T(8,128)} %bitcast.6, f32[1,4,8,1024]{3,2,1,0:T(8,128)} %bitcast.7, f32[16,128]{1,0:T(8,128)} %get-tuple-element.19.packed), custom_call_target="tpu_custom_call" | custom-call | tf_op jit(solution)/shard_map/finish/pallas_call | solution.py:673

commit v5 on v4

--- a/solution.py
+++ b/solution.py
@@ -373,9 +373,6 @@
     recv[me] = send[me]
     recv_extra[me] = send_extra[me]
     own[...] = jnp.zeros_like(own)
-    first_cat[...] = build_first(w_first[...], b_first[...])
-    second_cat[...], second_t[...] = build_second(w_second[...])
-    gather_first[...], gather_second[...] = build_gather()
     pl.semaphore_wait(pltpu.get_barrier_semaphore(), GROUP - 1 + 2 * SUBS - 1)
 
     def remote(src, dst, send_sem, recv_sem, target):
@@ -405,6 +402,9 @@
     for p in range(1, GROUP):
         extra_copy(group_target(p), me).start()
         data_copy(group_target(p), me).start()
+
+    first_cat[...] = build_first(w_first[...], b_first[...])
+    second_cat[...], second_t[...] = build_second(w_second[...])
 
     def two_senders(p, carry):
         for q in range(2):
@@ -511,6 +511,7 @@
     for i in range(DEPTH):
         place(i + 2, own[i])
     lax.fori_loop(2, 4, forward, 0)
+    gather_first[...], gather_second[...] = build_gather()
     finished(part_copy, SUBS)
     total = eighths[0]
     for s in range(1, SUBS):
@@ -556,7 +557,7 @@
         acc_first[:, :PATCH] += dot_nt(grad, patch_u[j])
         return carry
 
-    lax.fori_loop(0, 6, backward, 0, unroll=2)
+    lax.fori_loop(0, 6, backward, 0, unroll=3)
 
     packed = gathered(acc_first[...], gather_first[...])
     packed = packed + gathered(acc_second[...], gather_second[...])
@@ -565,6 +566,13 @@
     packed = packed + jnp.where((row == 0) & (lane == 60), jnp.sum(sum_square) / CELLS, 0.0)
     packed = packed + jnp.where((row == 0) & (lane == 61), jnp.sum(sum_resid), 0.0)
 
+    mine[1] = packed
+    whole_slots[pair] = packed
+    started(pair_copy, 2 * SUBS)
+    finished(pair_copy, 2 * SUBS)
+    packed = whole_slots[0]
+    for s in range(1, 16):
+        packed = packed + whole_slots[s]
     mine[0] = packed
     part_slots[slab] = packed
     started(slab_copy, SLABS)
@@ -572,13 +580,6 @@
     packed = part_slots[0]
     for s in range(1, 16):
         packed = packed + part_slots[s]
-    mine[1] = packed
-    whole_slots[pair] = packed
-    started(pair_copy, 2 * SUBS)
-    finished(pair_copy, 2 * SUBS)
-    packed = whole_slots[0]
-    for s in range(1, 16):
-        packed = packed + whole_slots[s]
     grads_out[...] = packed
 
     def sent(p, carry):

time: 61.2 us -> 59.7 us (0.975)
  Pallas kernels: 59.7 us -> 58.2 us
    pallas_call x1, Pallas kernels: 57.4 us -> 55.9 us  [body(): pl.pallas_call(step_kernel, name='train_step', out_shape=(shape((DEPTH, Y...]
where the time goes in v5:
time: 59.7 us; the launch traced here: 59.5 us
  Pallas kernels  58.2 us (97%)
  between operations  1.29 us (2%)
    pallas_call x1, Pallas kernels, body(): pl.pallas_call(step_kernel, name='train_step', out_shape=(shape((DEPTH, Y...  55.9 us
    pallas_call x1, Pallas kernels, body(): pl.pallas_call(finish_kernel, name='finish', out_shape=(shape((1, DEPTH,...  2.3 us

profile of v5, /device:TPU:1, one launch (start us, length us, event | category | flops | bytes accessed | tf_op | source)
XLA Modules:
  0.0 59.5 jit_solution(15996592257420833688)
XLA Ops:
  1.3 55.9 %train_step.1 = (f32[4,8,1024]{2,1,0:T(8,128)}, f32[4,8,1024]{2,1,0:T(8,128)}, f32[16,128]{1,0:T(8,128)}) custom-call(bf16[2,128,2048]{2,1,0:T(8,128)(2,1)} %sino.1, f32[2]{0:T(128)} %angles.1, f32[32,27]{1,0:T(8,128)} %w_first.1, f32[1,32]{1,0:T(1,128)} %bitcast.8, f32[32,27]{1,0:T(8,128)} %w_second.1, f32[1]{0:T(128)S(6)} %copy.13.b_second), custom_call_target="tpu_custom_call" | custom-call | tf_op jit(solution)/shard_map/train_step/pallas_call | solution.py:627
  57.2 2.3 %finish.1 = (f32[1,4,8,1024]{3,2,1,0:T(8,128)}, f32[1,4,8,1024]{3,2,1,0:T(8,128)}, f32[1,1]{1,0:T(1,128)}, f32[32,27]{1,0:T(8,128)}, f32[1,32]{1,0:T(1,128)}, /*index=5*/f32[32,27]{1,0:T(8,128)}, f32[1,1]{1,0:T(1,128)}) custom-call(f32[1,4,8,1024]{3,2,1,0:T(8,128)} %bitcast.6, f32[1,4,8,1024]{3,2,1,0:T(8,128)} %bitcast.7, f32[16,128]{1,0:T(8,128)} %get-tuple-element.19.packed), custom_call_target="tpu_custom_call" | custom-call | tf_op jit(solution)/shard_map/finish/pallas_call | solution.py:674

commit v6 on v5

--- a/solution.py
+++ b/solution.py
@@ -317,7 +317,7 @@
         if p < 8:
             return p & 1, p >> 1, 0
         q = p - 8
-        return (q // 3) & 1, q // 6, far_first[q % 3]
+        return (q // 3) & 1, 3 - q // 6, (1, 3, 2)[q % 3]
 
     def group_target(p):
         core, y, z = distance(p)
@@ -328,8 +328,8 @@
         third = lax.rem(q, 3)
         near = p < 8
         core = jnp.where(near, p, q // 3) & 1
-        y = jnp.where(near, p >> 1, q // 6)
-        z = jnp.where(near, 0, jnp.where(third == 0, 2, jnp.where(third == 1, 1, 3)))
+        y = jnp.where(near, p >> 1, 3 - q // 6)
+        z = jnp.where(near, 0, jnp.where(third == 0, 1, jnp.where(third == 1, 3, 2)))
         row = ((slab >> 2) + 4 - y) & 3
         return ((half + core) & 1) * SLABS + row * 4 + ((slab + 4 - z) & 3)
 

time: 59.7 us -> 58.7 us (0.983)
  Pallas kernels: 58.2 us -> 57.2 us
    pallas_call x1, Pallas kernels: 55.9 us -> 54.9 us  [body(): pl.pallas_call(step_kernel, name='train_step', out_shape=(shape((DEPTH, Y...]
where the time goes in v6:
time: 58.7 us; the launch traced here: 58.5 us
  Pallas kernels  57.2 us (97%)
  between operations  1.29 us (2%)
    pallas_call x1, Pallas kernels, body(): pl.pallas_call(step_kernel, name='train_step', out_shape=(shape((DEPTH, Y...  54.9 us
    pallas_call x1, Pallas kernels, body(): pl.pallas_call(finish_kernel, name='finish', out_shape=(shape((1, DEPTH,...  2.3 us

profile of v6, /device:TPU:1, one launch (start us, length us, event | category | flops | bytes accessed | tf_op | source)
XLA Modules:
  0.0 58.5 jit_solution(6017527051982432217)
XLA Ops:
  1.3 54.9 %train_step.1 = (f32[4,8,1024]{2,1,0:T(8,128)}, f32[4,8,1024]{2,1,0:T(8,128)}, f32[16,128]{1,0:T(8,128)}) custom-call(bf16[2,128,2048]{2,1,0:T(8,128)(2,1)} %sino.1, f32[2]{0:T(128)} %angles.1, f32[32,27]{1,0:T(8,128)} %w_first.1, f32[1,32]{1,0:T(1,128)} %bitcast.8, f32[32,27]{1,0:T(8,128)} %w_second.1, f32[1]{0:T(128)S(6)} %copy.13.b_second), custom_call_target="tpu_custom_call" | custom-call | tf_op jit(solution)/shard_map/train_step/pallas_call | solution.py:627
  56.2 2.3 %finish.1 = (f32[1,4,8,1024]{3,2,1,0:T(8,128)}, f32[1,4,8,1024]{3,2,1,0:T(8,128)}, f32[1,1]{1,0:T(1,128)}, f32[32,27]{1,0:T(8,128)}, f32[1,32]{1,0:T(1,128)}, /*index=5*/f32[32,27]{1,0:T(8,128)}, f32[1,1]{1,0:T(1,128)}) custom-call(f32[1,4,8,1024]{3,2,1,0:T(8,128)} %bitcast.6, f32[1,4,8,1024]{3,2,1,0:T(8,128)} %bitcast.7, f32[16,128]{1,0:T(8,128)} %get-tuple-element.19.packed), custom_call_target="tpu_custom_call" | custom-call | tf_op jit(solution)/shard_map/finish/pallas_call | solution.py:674

commit v7 on v6

--- a/solution.py
+++ b/solution.py
@@ -570,16 +570,12 @@
     whole_slots[pair] = packed
     started(pair_copy, 2 * SUBS)
     finished(pair_copy, 2 * SUBS)
-    packed = whole_slots[0]
-    for s in range(1, 16):
-        packed = packed + whole_slots[s]
+    packed = jnp.sum(whole_slots[...], axis=0)
     mine[0] = packed
     part_slots[slab] = packed
     started(slab_copy, SLABS)
     finished(slab_copy, SLABS)
-    packed = part_slots[0]
-    for s in range(1, 16):
-        packed = packed + part_slots[s]
+    packed = jnp.sum(part_slots[...], axis=0)
     grads_out[...] = packed
 
     def sent(p, carry):

time: 58.7 us -> 58.7 us (level)
  no operation moved by 1% of the time
where the time goes in v7:
time: 58.7 us; the launch traced here: 58.5 us
  Pallas kernels  57.2 us (97%)
  between operations  1.29 us (2%)
    pallas_call x1, Pallas kernels, body(): pl.pallas_call(step_kernel, name='train_step', out_shape=(shape((DEPTH, Y...  54.9 us
    pallas_call x1, Pallas kernels, body(): pl.pallas_call(finish_kernel, name='finish', out_shape=(shape((1, DEPTH,...  2.3 us

profile of v7, /device:TPU:1, one launch (start us, length us, event | category | flops | bytes accessed | tf_op | source)
XLA Modules:
  0.0 58.5 jit_solution(1514820517399998439)
XLA Ops:
  1.3 54.9 %train_step.1 = (f32[4,8,1024]{2,1,0:T(8,128)}, f32[4,8,1024]{2,1,0:T(8,128)}, f32[16,128]{1,0:T(8,128)}) custom-call(bf16[2,128,2048]{2,1,0:T(8,128)(2,1)} %sino.1, f32[2]{0:T(128)} %angles.1, f32[32,27]{1,0:T(8,128)} %w_first.1, f32[1,32]{1,0:T(1,128)} %bitcast.8, f32[32,27]{1,0:T(8,128)} %w_second.1, f32[1]{0:T(128)S(6)} %copy.13.b_second), custom_call_target="tpu_custom_call" | custom-call | tf_op jit(solution)/shard_map/train_step/pallas_call | solution.py:623
  56.2 2.3 %finish.1 = (f32[1,4,8,1024]{3,2,1,0:T(8,128)}, f32[1,4,8,1024]{3,2,1,0:T(8,128)}, f32[1,1]{1,0:T(1,128)}, f32[32,27]{1,0:T(8,128)}, f32[1,32]{1,0:T(1,128)}, /*index=5*/f32[32,27]{1,0:T(8,128)}, f32[1,1]{1,0:T(1,128)}) custom-call(f32[1,4,8,1024]{3,2,1,0:T(8,128)} %bitcast.6, f32[1,4,8,1024]{3,2,1,0:T(8,128)} %bitcast.7, f32[16,128]{1,0:T(8,128)} %get-tuple-element.19.packed), custom_call_target="tpu_custom_call" | custom-call | tf_op jit(solution)/shard_map/finish/pallas_call | solution.py:670
